TPU v7x, 512 devices: a whole 4x4x16 slice. The times are simulated.
512 devices in a mesh: gx: 32 (over z, core), gy: 16 (over y, x).
Axes of the slice: x: 4, y: 4, z: 16, core: 2. Of those that a mesh axis runs over, the one named last changes fastest.
Arguments:
- source: float32 [32, 4096, 2048], P(None, 'gx', 'gy'), may hold values from -6 to 6
- stretch_index: int32 [2048], replicated, may hold values from 0 to 8, as said below
- mode_index: int32 [512], replicated, may hold values from 0 to 2047, as said below
Outputs:
- pressure_modes: float32 [2, 32, 512, 2048], P(None, None, 'gx', 'gy')
Inputs may be any that keep to these rules, and one draw needn't show every extreme that they name: `stretch_index`: 0 at both walls and 8 at the two centre cells; neighbouring cells differ by at most one. `mode_index`: 512 distinct wavenumbers; 0 and 2047 are always among them.
All inputs are finite; a program needn't handle non-finite values.
Results may differ from a plain program's by a relative error of at most 0.0017.
Values sent between devices are 32-bit elements; how exact they have to be, the bound alone decides.
No kernel may reach another device: no remote copies, remote signals or barrier semaphores. Data moves between devices by JAX's collectives and lax.ppermute only.
A program may use at most 64 MiB of HBM per device.

v0:
```python
import math

import jax
import jax.numpy as jnp
from jax import lax
from jax.sharding import PartitionSpec as P


def from_behind(block, axis, distance):
    devices = range(lax.axis_size(axis))
    route = [(i - distance, i) for i in devices if i - distance in devices]
    return lax.ppermute(block, axis, route)


def spacing_bands(stretch_index):
    spacing = 0.25 * jnp.exp2(0.25 * stretch_index.astype(jnp.float32))
    faces = 0.5 * (spacing[:-1] + spacing[1:])
    zeros_one = jnp.zeros((1,), jnp.float32)
    lower_band = jnp.concatenate([zeros_one, 1.0 / (spacing[1:] * faces)])
    upper_band = jnp.concatenate([1.0 / (spacing[:-1] * faces), zeros_one])
    return (lower_band, upper_band)


def shift_terms(mode_values, plane_count, stream_length):
    stream_wave = mode_values.astype(jnp.float32) * (2.0 * math.pi / stream_length)
    span_wave = 0.04 * (jnp.arange(plane_count, dtype=jnp.float32) + 1.0)
    return span_wave[:, None] * span_wave[:, None] + stream_wave[None, :] * stream_wave[None, :]


def earlier_rows(values, distance, fill):
    padding = jnp.full(values.shape[:-1] + (distance,), fill, values.dtype)
    return jnp.concatenate([padding, values[..., :-distance]], -1)


def later_rows(values, distance, fill):
    padding = jnp.full(values.shape[:-1] + (distance,), fill, values.dtype)
    return jnp.concatenate([values[..., distance:], padding], -1)


def reduce_cyclic(lower_band, diagonal, upper_band, right_side):
    lower_band = jnp.broadcast_to(lower_band, diagonal.shape)
    upper_band = jnp.broadcast_to(upper_band, diagonal.shape)
    extent = diagonal.shape[-1]
    distance = 1
    while distance < extent:
        factor_low = lower_band / earlier_rows(diagonal, distance, 1.0)
        factor_up = upper_band / later_rows(diagonal, distance, 1.0)
        new_diagonal = (
            diagonal
            - factor_low * earlier_rows(upper_band, distance, 0.0)
            - factor_up * later_rows(lower_band, distance, 0.0)
        )
        right_side = (
            right_side
            - factor_low * earlier_rows(right_side, distance, 0.0)
            - factor_up * later_rows(right_side, distance, 0.0)
        )
        lower_band = -factor_low * earlier_rows(lower_band, distance, 0.0)
        upper_band = -factor_up * later_rows(upper_band, distance, 0.0)
        diagonal = new_diagonal
        distance = distance * 2
    return right_side / diagonal


def transform(pencils, mode_index, stream_length):
    mode_total = mode_index.shape[0]
    block_size = 256
    positions = jnp.arange(stream_length, dtype=jnp.int32)
    groups = mode_index.reshape(mode_total // block_size, block_size)

    def per_block(mode_block):
        phases = (mode_block[:, None] * positions[None, :] % stream_length).astype(jnp.float32) * (
            2.0 * math.pi / stream_length
        )
        cosine_table = jnp.cos(phases)
        sine_table = jnp.sin(phases)
        real_part = jnp.einsum(
            "kx,zxy->zky", cosine_table, pencils, precision=lax.Precision.HIGHEST
        )
        imag_part = -jnp.einsum("kx,zxy->zky", sine_table, pencils, precision=lax.Precision.HIGHEST)
        return jnp.stack([real_part, imag_part])

    stacked = lax.map(per_block, groups)
    stacked = jnp.moveaxis(stacked, 0, 2)
    shaped = stacked.reshape(2, pencils.shape[0], mode_total, pencils.shape[2])
    return shaped * (1.0 / math.sqrt(stream_length))


def doubling(reduced, gy_index, gy_count):
    lower_band, diagonal, upper_band, right_side = (
        reduced[0],
        reduced[1],
        reduced[2],
        reduced[3:5],
    )
    distance = 1
    while distance < gy_count:
        packed = jnp.concatenate([jnp.stack([lower_band, diagonal, upper_band]), right_side], 0)
        beneath = from_behind(packed, "gy", distance)
        higher = from_behind(packed, "gy", -distance)
        beneath_diagonal = jnp.where(gy_index >= distance, beneath[1], 1.0)
        higher_diagonal = jnp.where(gy_index + distance < gy_count, higher[1], 1.0)
        factor_low = lower_band / beneath_diagonal
        factor_up = upper_band / higher_diagonal
        new_diagonal = diagonal - factor_low * beneath[2] - factor_up * higher[0]
        right_side = right_side - factor_low * beneath[3:5] - factor_up * higher[3:5]
        lower_band = -factor_low * beneath[0]
        upper_band = -factor_up * higher[2]
        diagonal = new_diagonal
        distance = distance * 2
    own_value = right_side / diagonal
    before_value = from_behind(own_value, "gy", 1)
    return (own_value, before_value)


def local(source, stretch_index, mode_index):
    gx_count = lax.axis_size("gx")
    gy_count = lax.axis_size("gy")
    planes, stream_rows, wall_rows = source.shape
    stream_length = stream_rows * gx_count
    mode_count = mode_index.shape[0] // gx_count
    gx_index = lax.axis_index("gx")
    gy_index = lax.axis_index("gy")
    pencils = lax.all_to_all(source, "gx", split_axis=0, concat_axis=1, tiled=True)
    spectra = transform(pencils, mode_index, stream_length)
    lower_all, upper_all = spacing_bands(stretch_index)
    own_modes = lax.dynamic_slice_in_dim(mode_index, gx_index * mode_count, mode_count)
    blocks = lax.all_to_all(spectra, "gx", split_axis=2, concat_axis=1, tiled=True)
    row_ids = jnp.arange(wall_rows)
    last_row = wall_rows - 1
    row_start = gy_index * wall_rows
    lower_band = lax.dynamic_slice_in_dim(lower_all, row_start, wall_rows)
    upper_band = lax.dynamic_slice_in_dim(upper_all, row_start, wall_rows)
    terms = shift_terms(own_modes, planes, stream_length)
    diagonal = lower_band + upper_band + terms[..., None]
    sys_lower = jnp.where((row_ids == 0) | (row_ids == last_row), 0.0, -lower_band)
    sys_upper = jnp.where(row_ids >= last_row - 1, 0.0, -upper_band)
    sys_diagonal = jnp.where(row_ids == last_row, 1.0, diagonal)
    left_term = jnp.broadcast_to(jnp.where(row_ids == 0, lower_band, 0.0), diagonal.shape)
    right_term = jnp.broadcast_to(
        jnp.where(row_ids == last_row - 1, upper_band, 0.0), diagonal.shape
    )
    inner_side = jnp.where(row_ids == last_row, 0.0, blocks)
    right_side = jnp.concatenate([inner_side, left_term[None], right_term[None]], 0)
    solved = reduce_cyclic(sys_lower, sys_diagonal, sys_upper, right_side)
    particular = solved[:2]
    from_left = solved[2]
    from_right = solved[3]
    first_rows = jnp.stack(
        [particular[0, ..., 0], particular[1, ..., 0], from_left[..., 0], from_right[..., 0]]
    ).reshape(4, -1)
    following = from_behind(first_rows, "gy", -1).reshape(4, planes, mode_count)
    a_sep = lower_band[last_row]
    c_sep = upper_band[last_row]
    coupling_low = -a_sep * from_left[..., last_row - 1]
    coupling_mid = (
        diagonal[..., last_row] - a_sep * from_right[..., last_row - 1] - c_sep * following[2]
    )
    coupling_high = -c_sep * following[3]
    source_sep = (
        blocks[..., last_row] + a_sep * particular[..., last_row - 1] + c_sep * following[0:2]
    )
    reduced = jnp.concatenate(
        [jnp.stack([coupling_low, coupling_mid, coupling_high]), source_sep], 0
    ).reshape(5, -1)
    own_value, before_value = doubling(reduced, gy_index, gy_count)
    own_value = own_value.reshape(2, planes, mode_count)
    before_value = before_value.reshape(2, planes, mode_count)
    result = particular + before_value[..., None] * from_left + own_value[..., None] * from_right
    return jnp.where(row_ids == last_row, own_value[..., None], result)


def solution(mesh):
    in_specs = (P(None, "gx", "gy"), P(), P())
    out_specs = P(None, None, "gx", "gy")
    return jax.shard_map(local, mesh=mesh, in_specs=in_specs, out_specs=out_specs, check_vma=False)
```

profile of v0, /device:TPU:24, one launch (start us, length us, event | category | flops | bytes accessed | tf_op | source)
XLA Modules:
  0.0 326.1 jit_solution(656380435173947116)
XLA Ops:
  0.0 15.7 %all-to-all-start = ((f32[32,128,128]{2,1,0:T(8,128)}), f32[32,128,128]{2,1,0:T(8,128)}, u32[]{:S(2)}, u32[]{:S(2)}) async-start(f32[32,128,128]{2,1,0:T(8,128)} %param.5), calls=%async_computation | async-start | bytes 4194304 | tf_op jit(solution)/shard_map/all_to_all | solution.py:124
  16.9 0.9 multiply_subtract_fusion.12
  20.5 0.8 fusion.97
  21.7 93.2 %all-to-all-done = f32[32,128,128]{2,1,0:T(8,128)} async-done(((f32[32,128,128]{2,1,0:T(8,128)}), f32[32,128,128]{2,1,0:T(8,128)}, u32[]{:S(2)}, u32[]{:S(2)}) %all-to-all-start) | async-done | bytes 2097184 | tf_op jit(solution)/shard_map/all_to_all | solution.py:124
  115.0 101.3 %while.13 = (s32[]{:T(128)}, f32[2,2,1,256,128]{4,3,0,1,2:T(8,128)}, s32[2,256]{1,0:T(2,128)S(1)}, f32[1,4096,128]{2,1,0:T(8,128)}, s32[]{:T(128)}) while((s32[]{:T(128)}, f32[2,2,1,256,128]{4,3,0,1,2:T(8,128)}, s32[2,256]{1,0:T(2,128)S(1)}, f32[1,4096,128]{2,1,0:T(8,128)}, s32[]{:T(128)}) %tuple.91), condition=%wide.region_1.2_spmd.clone, body=%wide.region_0.1_spmd.clone.sunk | while | flops 3250683904 | bytes 9179269 | solution.py:83
  115.4 20.6 %fusion.125 = f32[1,1,256,128]{3,2,1,0:T(8,128)S(1)} fusion(f32[1,4096,128]{2,1,0:T(8,128)} %get-tuple-element.246, s32[256]{0:T(256)S(1)} %bitcast.69), kind=kOutput, calls=%fused_computation.19.clone.1 | convolution fusion | flops 1625325568 | bytes 2229248 | tf_op jit(solution)/shard_map/while/body/eval_jaxpr/kx,zxy->zky/dot_general | solution.py:80
  136.0 20.9 %fusion.126 = f32[1,1,256,128]{3,2,1,0:T(8,128)S(1)} fusion(f32[1,4096,128]{2,1,0:T(8,128)} %get-tuple-element.246, s32[256]{0:T(256)S(1)} %bitcast.70), kind=kOutput, calls=%fused_computation.17.clone.1 | convolution fusion | flops 1625292800 | bytes 2229248 | tf_op jit(solution)/shard_map/while/body/eval_jaxpr/kx,zxy->zky/dot_general | solution.py:77
  157.0 0.8 copy-done.10
  162.3 20.6 %fusion.125 = f32[1,1,256,128]{3,2,1,0:T(8,128)S(1)} fusion(f32[1,4096,128]{2,1,0:T(8,128)} %get-tuple-element.246, s32[256]{0:T(256)S(1)} %bitcast.69), kind=kOutput, calls=%fused_computation.19.clone.1 | convolution fusion | flops 1625325568 | bytes 2229248 | tf_op jit(solution)/shard_map/while/body/eval_jaxpr/kx,zxy->zky/dot_general | solution.py:80
  182.9 20.9 %fusion.126 = f32[1,1,256,128]{3,2,1,0:T(8,128)S(1)} fusion(f32[1,4096,128]{2,1,0:T(8,128)} %get-tuple-element.246, s32[256]{0:T(256)S(1)} %bitcast.70), kind=kOutput, calls=%fused_computation.17.clone.1 | convolution fusion | flops 1625292800 | bytes 2229248 | tf_op jit(solution)/shard_map/while/body/eval_jaxpr/kx,zxy->zky/dot_general | solution.py:77
  203.9 0.8 copy-done.10
  216.3 1.1 broadcast_multiply_fusion
  217.4 1.2 copy.6
  218.6 4.7 %all-to-all-start.1 = ((f32[2,1,512,128]{3,0,1,2:T(2,128)}), f32[2,1,512,128]{3,0,1,2:T(2,128)}, u32[]{:S(2)}, u32[]{:S(2)}) async-start(f32[2,1,512,128]{3,0,1,2:T(2,128)} %copy.6), calls=%async_computation.1 | async-start | bytes 1048576 | tf_op jit(solution)/shard_map/all_to_all | solution.py:128
  223.2 0.9 fusion.98
  224.1 0.6 slice.332
  224.7 0.6 slice.388
  225.3 0.9 fusion.96
  226.2 0.9 pad_multiply_fusion.1
  227.1 0.8 slice.484
  229.2 1.0 pad_multiply_fusion.2
  230.4 1.2 multiply_subtract_fusion.7
  231.6 0.7 copy-done.2
  232.5 1.1 multiply_subtract_fusion.6
  233.6 23.4 %all-to-all-done.1 = f32[2,1,512,128]{3,0,1,2:T(2,128)} async-done(((f32[2,1,512,128]{3,0,1,2:T(2,128)}), f32[2,1,512,128]{3,0,1,2:T(2,128)}, u32[]{:S(2)}, u32[]{:S(2)}) %all-to-all-start.1) | async-done | bytes 524320 | tf_op jit(solution)/shard_map/all_to_all | solution.py:128
  257.0 1.1 fusion.93
  262.6 0.6 copy-done.1
  264.1 0.6 copy-done.4
  265.7 1.0 fusion.45
  267.4 4.8 %collective-permute-start = (f32[4,512]{1,0:T(4,128)S(1)}, f32[4,512]{1,0:T(4,128)S(1)}, u32[]{:S(2)}, u32[]{:S(2)}) collective-permute-start(f32[4,512]{1,0:T(4,128)S(1)} %pad_maximum_fusion.5), channel_id=1, source_target_pairs={{1,0},{2,1},{3,2},{4,3},{5,4},{6,5},{7,6},{8,7},{9,8},{10,9},{11,1... | collective-permute-start | bytes 24584 | tf_op jit(solution)/shard_map/ppermute | solution.py:12
  272.3 1.1 fusion.43
  273.6 0.7 fusion.56
  274.3 0.7 fusion.73
  275.0 2.7 collective-permute-start.1
  277.7 5.5 %collective-permute-start.2 = (f32[5,512]{1,0:T(8,128)S(1)}, f32[5,512]{1,0:T(8,128)S(1)}, u32[]{:S(2)}, u32[]{:S(2)}) collective-permute-start(f32[5,512]{1,0:T(8,128)S(1)} %pad_maximum_fusion.1), channel_id=1, source_target_pairs={{1,0},{2,1},{3,2},{4,3},{5,4},{6,5},{7,6},{8,7},{9,8},{10,9},{11,1... | collective-permute-start | bytes 30728 | tf_op jit(solution)/shard_map/ppermute | solution.py:12
  283.3 1.4 collective-permute-done.2
  284.7 2.2 collective-permute-start.3
  286.9 6.1 %collective-permute-start.4 = (f32[5,512]{1,0:T(8,128)S(1)}, f32[5,512]{1,0:T(8,128)S(1)}, u32[]{:S(2)}, u32[]{:S(2)}) collective-permute-start(f32[5,512]{1,0:T(8,128)S(1)} %pad_maximum_fusion.2), channel_id=1, source_target_pairs={{2,0},{3,1},{4,2},{5,3},{6,4},{7,5},{8,6},{9,7},{10,8},{11,9},{12,... | collective-permute-start | bytes 30728 | tf_op jit(solution)/shard_map/ppermute | solution.py:12
  293.0 1.4 collective-permute-done.4
  294.5 1.3 collective-permute-start.5
  295.8 6.2 %collective-permute-start.6 = (f32[5,512]{1,0:T(8,128)S(1)}, f32[5,512]{1,0:T(8,128)S(1)}, u32[]{:S(2)}, u32[]{:S(2)}) collective-permute-start(f32[5,512]{1,0:T(8,128)S(1)} %pad_maximum_fusion.3), channel_id=1, source_target_pairs={{4,0},{5,1},{6,2},{7,3},{8,4},{9,5},{10,6},{11,7},{12,8},{13,9},{1... | collective-permute-start | bytes 30728 | tf_op jit(solution)/shard_map/ppermute | solution.py:12
  302.1 1.4 collective-permute-done.6
  303.5 6.3 %collective-permute-start.8 = (f32[5,512]{1,0:T(8,128)S(1)}, f32[5,512]{1,0:T(8,128)S(1)}, u32[]{:S(2)}, u32[]{:S(2)}) collective-permute-start(f32[5,512]{1,0:T(8,128)S(1)} %pad_maximum_fusion.4), channel_id=1, source_target_pairs={{8,0},{9,1},{10,2},{11,3},{12,4},{13,5},{14,6},{15,7},{24,16},{25,... | collective-permute-start | bytes 30728 | tf_op jit(solution)/shard_map/ppermute | solution.py:12
  309.8 1.3 collective-permute-start.7
  311.2 5.7 %collective-permute-done.7 = f32[5,512]{1,0:T(8,128)S(1)} collective-permute-done((f32[5,512]{1,0:T(8,128)S(1)}, f32[5,512]{1,0:T(8,128)S(1)}, u32[]{:S(2)}, u32[]{:S(2)}) %collective-permute-start.7) | collective-permute-done | bytes 10272 | tf_op jit(solution)/shard_map/ppermute | solution.py:12
  317.0 3.4 %collective-permute-start.9 = (f32[2,512]{1,0:T(2,128)S(1)}, f32[2,512]{1,0:T(2,128)S(1)}, u32[]{:S(2)}, u32[]{:S(2)}) collective-permute-start(f32[2,512]{1,0:T(2,128)S(1)} %fusion.48), channel_id=1, source_target_pairs={{0,1},{1,2},{2,3},{3,4},{4,5},{5,6},{6,7},{7,8},{8,9},{9,10},{10,1... | collective-permute-start | bytes 12296 | tf_op jit(solution)/shard_map/ppermute | solution.py:12
  320.5 4.1 %collective-permute-done.9 = f32[2,512]{1,0:T(2,128)S(1)} collective-permute-done((f32[2,512]{1,0:T(2,128)S(1)}, f32[2,512]{1,0:T(2,128)S(1)}, u32[]{:S(2)}, u32[]{:S(2)}) %collective-permute-start.9) | collective-permute-done | bytes 4128 | tf_op jit(solution)/shard_map/ppermute | solution.py:12
  324.7 1.1 fusion.41
  (127 shorter events, 12.2 us)
Async XLA Ops:
  0.0 15.8 %copy-start.11 = (s32[2048]{0:T(1024)S(1)}, s32[2048]{0:T(1024)}, u32[]{:S(2)}) copy-start(s32[2048]{0:T(1024)} %param.6) | copy-start | bytes 24580
  0.0 15.9 %copy-start.12 = (s32[512]{0:T(512)S(1)}, s32[512]{0:T(512)}, u32[]{:S(2)}) copy-start(s32[512]{0:T(512)} %param.7) | copy-start | bytes 6148
  0.0 115.0 %all-to-all-start = ((f32[32,128,128]{2,1,0:T(8,128)}), f32[32,128,128]{2,1,0:T(8,128)}, u32[]{:S(2)}, u32[]{:S(2)}) async-start(f32[32,128,128]{2,1,0:T(8,128)} %param.5), calls=%async_computation | async-start | bytes 4194304 | tf_op jit(solution)/shard_map/all_to_all | solution.py:124
  136.0 21.0 %copy-start.9 = (f32[2,2,1,256,128]{4,3,0,1,2:T(8,128)S(1)}, f32[2,2,1,256,128]{4,3,0,1,2:T(8,128)}, u32[]{:S(2)}) copy-start(f32[2,2,1,256,128]{4,3,0,1,2:T(8,128)} %get-tuple-element.239) | copy-start | bytes 1572868 | tf_op jit(solution)/shard_map/while
  157.0 0.8 copy-start.10
  182.9 20.9 %copy-start.9 = (f32[2,2,1,256,128]{4,3,0,1,2:T(8,128)S(1)}, f32[2,2,1,256,128]{4,3,0,1,2:T(8,128)}, u32[]{:S(2)}) copy-start(f32[2,2,1,256,128]{4,3,0,1,2:T(8,128)} %get-tuple-element.239) | copy-start | bytes 1572868 | tf_op jit(solution)/shard_map/while
  203.9 0.8 copy-start.10
  218.6 38.4 %all-to-all-start.1 = ((f32[2,1,512,128]{3,0,1,2:T(2,128)}), f32[2,1,512,128]{3,0,1,2:T(2,128)}, u32[]{:S(2)}, u32[]{:S(2)}) async-start(f32[2,1,512,128]{3,0,1,2:T(2,128)} %copy.6), calls=%async_computation.1 | async-start | bytes 1048576 | tf_op jit(solution)/shard_map/all_to_all | solution.py:128
  227.1 3.3 %copy-start = (f32[32,16,128]{2,1,0:T(8,128)S(1)}, f32[32,16,128]{2,1,0:T(8,128)}, u32[]{:S(2)}) copy-start(f32[32,16,128]{2,1,0:T(8,128)} %get-tuple-element.115) | copy-start | bytes 786436
  230.4 2.1 copy-start.7
  231.6 0.7 copy-start.2
  262.2 1.0 copy-start.1
  262.2 1.0 copy-start.3
  263.7 1.0 copy-start.4
  263.7 1.0 copy-start.5
  263.7 1.1 copy-start.6
  264.8 0.9 copy-start.8
  267.4 6.2 %collective-permute-start = (f32[4,512]{1,0:T(4,128)S(1)}, f32[4,512]{1,0:T(4,128)S(1)}, u32[]{:S(2)}, u32[]{:S(2)}) collective-permute-start(f32[4,512]{1,0:T(4,128)S(1)} %pad_maximum_fusion.5), channel_id=1, source_target_pairs={{1,0},{2,1},{3,2},{4,3},{5,4},{6,5},{7,6},{8,7},{9,8},{10,9},{11,1... | collective-permute-start | bytes 24584 | tf_op jit(solution)/shard_map/ppermute | solution.py:12
  275.0 8.2 %collective-permute-start.1 = (f32[5,512]{1,0:T(8,128)S(1)}, f32[5,512]{1,0:T(8,128)S(1)}, u32[]{:S(2)}, u32[]{:S(2)}) collective-permute-start(f32[5,512]{1,0:T(8,128)S(1)} %pad_maximum_fusion.1), channel_id=1, source_target_pairs={{0,1},{1,2},{2,3},{3,4},{4,5},{5,6},{6,7},{7,8},{8,9},{9,10},{10,1... | collective-permute-start | bytes 30728 | tf_op jit(solution)/shard_map/ppermute | solution.py:12
  277.7 6.9 %collective-permute-start.2 = (f32[5,512]{1,0:T(8,128)S(1)}, f32[5,512]{1,0:T(8,128)S(1)}, u32[]{:S(2)}, u32[]{:S(2)}) collective-permute-start(f32[5,512]{1,0:T(8,128)S(1)} %pad_maximum_fusion.1), channel_id=1, source_target_pairs={{1,0},{2,1},{3,2},{4,3},{5,4},{6,5},{7,6},{8,7},{9,8},{10,9},{11,1... | collective-permute-start | bytes 30728 | tf_op jit(solution)/shard_map/ppermute | solution.py:12
  284.7 8.3 %collective-permute-start.3 = (f32[5,512]{1,0:T(8,128)S(1)}, f32[5,512]{1,0:T(8,128)S(1)}, u32[]{:S(2)}, u32[]{:S(2)}) collective-permute-start(f32[5,512]{1,0:T(8,128)S(1)} %pad_maximum_fusion.2), channel_id=1, source_target_pairs={{0,2},{1,3},{2,4},{3,5},{4,6},{5,7},{6,8},{7,9},{8,10},{9,11},{10,... | collective-permute-start | bytes 30728 | tf_op jit(solution)/shard_map/ppermute | solution.py:12
  286.9 7.5 %collective-permute-start.4 = (f32[5,512]{1,0:T(8,128)S(1)}, f32[5,512]{1,0:T(8,128)S(1)}, u32[]{:S(2)}, u32[]{:S(2)}) collective-permute-start(f32[5,512]{1,0:T(8,128)S(1)} %pad_maximum_fusion.2), channel_id=1, source_target_pairs={{2,0},{3,1},{4,2},{5,3},{6,4},{7,5},{8,6},{9,7},{10,8},{11,9},{12,... | collective-permute-start | bytes 30728 | tf_op jit(solution)/shard_map/ppermute | solution.py:12
  294.5 7.5 %collective-permute-start.5 = (f32[5,512]{1,0:T(8,128)S(1)}, f32[5,512]{1,0:T(8,128)S(1)}, u32[]{:S(2)}, u32[]{:S(2)}) collective-permute-start(f32[5,512]{1,0:T(8,128)S(1)} %pad_maximum_fusion.3), channel_id=1, source_target_pairs={{0,4},{1,5},{2,6},{3,7},{4,8},{5,9},{6,10},{7,11},{8,12},{9,13},{1... | collective-permute-start | bytes 30728 | tf_op jit(solution)/shard_map/ppermute | solution.py:12
  295.8 7.6 %collective-permute-start.6 = (f32[5,512]{1,0:T(8,128)S(1)}, f32[5,512]{1,0:T(8,128)S(1)}, u32[]{:S(2)}, u32[]{:S(2)}) collective-permute-start(f32[5,512]{1,0:T(8,128)S(1)} %pad_maximum_fusion.3), channel_id=1, source_target_pairs={{4,0},{5,1},{6,2},{7,3},{8,4},{9,5},{10,6},{11,7},{12,8},{13,9},{1... | collective-permute-start | bytes 30728 | tf_op jit(solution)/shard_map/ppermute | solution.py:12
  303.5 7.7 %collective-permute-start.8 = (f32[5,512]{1,0:T(8,128)S(1)}, f32[5,512]{1,0:T(8,128)S(1)}, u32[]{:S(2)}, u32[]{:S(2)}) collective-permute-start(f32[5,512]{1,0:T(8,128)S(1)} %pad_maximum_fusion.4), channel_id=1, source_target_pairs={{8,0},{9,1},{10,2},{11,3},{12,4},{13,5},{14,6},{15,7},{24,16},{25,... | collective-permute-start | bytes 30728 | tf_op jit(solution)/shard_map/ppermute | solution.py:12
  309.8 7.1 %collective-permute-start.7 = (f32[5,512]{1,0:T(8,128)S(1)}, f32[5,512]{1,0:T(8,128)S(1)}, u32[]{:S(2)}, u32[]{:S(2)}) collective-permute-start(f32[5,512]{1,0:T(8,128)S(1)} %pad_maximum_fusion.4), channel_id=1, source_target_pairs={{0,8},{1,9},{2,10},{3,11},{4,12},{5,13},{6,14},{7,15},{16,24},{17,... | collective-permute-start | bytes 30728 | tf_op jit(solution)/shard_map/ppermute | solution.py:12
  317.0 7.6 %collective-permute-start.9 = (f32[2,512]{1,0:T(2,128)S(1)}, f32[2,512]{1,0:T(2,128)S(1)}, u32[]{:S(2)}, u32[]{:S(2)}) collective-permute-start(f32[2,512]{1,0:T(2,128)S(1)} %fusion.48), channel_id=1, source_target_pairs={{0,1},{1,2},{2,3},{3,4},{4,5},{5,6},{6,7},{7,8},{8,9},{9,10},{10,1... | collective-permute-start | bytes 12296 | tf_op jit(solution)/shard_map/ppermute | solution.py:12
where the time goes:
time: 330 us; the launch traced here: 326 us
  waiting for transfers between devices  131 us (40%)
  matrix products  83 us (25%)
  starting transfers between devices  60.2 us (18%)
  other arithmetic  17.7 us (5%)
  loops' own time  16.6 us (5%)
  local copies, waits for them, and re-layouts  15.5 us (5%)
    all_to_all x1, waiting for transfers between devices, local(): lax.all_to_all(source, 'gx', split_axis=0, concat_axis=1, tiled=True)  93.2 us
    dot_general x2, matrix products, per_block(): jnp.einsum('kx,zxy->zky', cosine_table, pencils, precision=lax.Precision....  41.9 us
    dot_general x2, matrix products, per_block(): jnp.einsum('kx,zxy->zky', sine_table, pencils, precision=lax.Precision.HI...  41.2 us
    ppermute x10, starting transfers between devices, from_behind(): return lax.ppermute(block, axis, route)  39.8 us
    all_to_all x1, waiting for transfers between devices, local(): lax.all_to_all(spectra, 'gx', split_axis=2, concat_axis=1, tiled=True)  23.4 us
    another operation x1, loops' own time, transform(): stacked = lax.map(per_block, groups)  16.6 us
    all_to_all x1, starting transfers between devices, local(): lax.all_to_all(source, 'gx', split_axis=0, concat_axis=1, tiled=True)  15.7 us
    ppermute x10, waiting for transfers between devices, from_behind(): return lax.ppermute(block, axis, route)  14.1 us
  transfers between devices with their start and end apart: 12, of which 8 were waited for; matrix products, arithmetic and copies ran while one was open for 5% of the time, Pallas kernels for 0%

commit v1 on v0

v1 whole, which is shorter than its diff:
```python
import functools
import math

import jax
import jax.numpy as jnp
from jax import lax
from jax.experimental import pallas as pl
from jax.experimental.pallas import tpu as pltpu
from jax.sharding import PartitionSpec as P

F32 = jnp.float32
BF16 = jnp.bfloat16
VMEM = pl.BlockSpec(memory_space=pltpu.VMEM)
SMEM = pl.BlockSpec(memory_space=pltpu.SMEM)
PARAMS = pltpu.CompilerParams(vmem_limit_bytes=48 * 1024 * 1024)


def spacing_bands(stretch_index):
    spacing = 0.25 * jnp.exp2(0.25 * stretch_index.astype(F32))
    faces = 0.5 * (spacing[:-1] + spacing[1:])
    zeros_one = jnp.zeros((1,), F32)
    lower_band = jnp.concatenate([zeros_one, 1.0 / (spacing[1:] * faces)])
    upper_band = jnp.concatenate([1.0 / (spacing[:-1] * faces), zeros_one])
    return (lower_band, upper_band)


def halves(values):
    high = values.astype(BF16)
    low = (values - high.astype(F32)).astype(BF16)
    return high, low


def table_kernel(length, starts_ref, modes_ref, high_ref, low_ref):
    quarter = length // 4
    mode_column = modes_ref[...]
    for side in range(2):
        place = starts_ref[side] + lax.broadcasted_iota(jnp.int32, (1, 128), 1)
        phase = (mode_column * place) & (length - 1)
        turn = (phase + quarter // 2) // quarter
        angle = (phase - turn * quarter).astype(F32) * (2.0 * math.pi / length)
        square = angle * angle
        sine = angle * (
            1.0
            + square
            * (-1.0 / 6 + square * (1.0 / 120 + square * (-1.0 / 5040 + square * (1.0 / 362880))))
        )
        cosine = 1.0 + square * (
            -0.5 + square * (1.0 / 24 + square * (-1.0 / 720 + square * (1.0 / 40320)))
        )
        odd = (turn & 1) == 1
        real = jnp.where(odd, sine, cosine)
        imag = jnp.where(odd, cosine, sine)
        scale = 1.0 / math.sqrt(length)
        real = jnp.where(((turn + 1) & 2) == 2, -scale, scale) * real
        imag = jnp.where((turn & 2) == 2, scale, -scale) * imag
        columns = pl.ds(side * 128, 128)
        for part, values in enumerate((real, imag)):
            high, low = halves(values)
            high_ref[:, part, :, columns] = high.reshape(-1, 16, 128)
            low_ref[:, part, :, columns] = low.reshape(-1, 16, 128)


def spectrum_kernel(core_ref, high_ref, low_ref, own_ref, got_ref, out_ref):
    del core_ref
    field = jnp.concatenate(
        [
            jnp.concatenate([own_ref[0], own_ref[1]], 1),
            jnp.concatenate([got_ref[0], got_ref[1]], 1),
        ],
        0,
    )
    field_high, field_low = halves(field)
    chips = out_ref.shape[0]
    step = 4
    for first in range(0, chips, step):
        rows = pl.ds(first * 64, step * 64)
        high = high_ref[rows, :]
        total = jnp.dot(high, field_high, preferred_element_type=F32)
        total += jnp.dot(high, field_low, preferred_element_type=F32)
        total += jnp.dot(low_ref[rows, :], field_high, preferred_element_type=F32)
        for plane in range(2):
            piece = total[:, plane * 128 : (plane + 1) * 128]
            out_ref[pl.ds(first, step), :, plane, :, :] = piece.reshape(step, 2, 32, 128)


def factor_kernel(
    info_ref,
    low_ref,
    up_ref,
    modes_ref,
    ratio_ref,
    inverse_ref,
    back_ref,
    left_ref,
    right_ref,
    carry_ref,
    corner,
):
    core = info_ref[0]
    block = info_ref[1]
    rows = 128
    blocks = carry_ref.shape[1] // 1
    sublane = lax.broadcasted_iota(jnp.int32, (8, 128), 0)
    lane = lax.broadcasted_iota(jnp.int32, (8, 128), 1)
    half = jnp.where(sublane < 4, core, 1 - core)
    plane = 16 * half + 4 * (sublane & 3) + lane // 32
    span_wave = 0.04 * (plane.astype(F32) + 1.0)
    stream_wave = modes_ref[...].astype(F32) * (2.0 * math.pi / 4096)
    shift = span_wave * span_wave + stream_wave * stream_wave

    group = 8
    for first in range(0, blocks, group):
        state = []
        for b in range(first, first + group):
            low, up = low_ref[b * rows], up_ref[b * rows]
            inverse = 1.0 / (low + up + shift)
            state.append((inverse, jnp.ones_like(shift), up * inverse, inverse))

        def forward(j, state):
            later = []
            for k in range(group):
                at = (first + k) * rows + j
                low, up, before = low_ref[at], up_ref[at], up_ref[at - 1]
                inverse, chain, product, corner_sum = state[k]
                ratio = low * inverse
                inverse = 1.0 / (low + up + shift - ratio * before)
                chain = chain * ratio
                corner_sum = corner_sum + product * (chain * inverse)
                later.append((inverse, chain, product * (up * inverse), corner_sum))
            return tuple(later)

        state = lax.fori_loop(1, rows, forward, tuple(state))
        for k in range(group):
            b = first + k
            inverse, chain, product, corner_sum = state[k]
            low, up = low_ref[b * rows], up_ref[b * rows + rows - 1]
            corner[0, b] = low * corner_sum
            corner[1, b] = low * (chain * inverse)
            corner[2, b] = product
            corner[3, b] = up * inverse

    reach = jnp.zeros_like(shift)
    for b in range(blocks):
        left_first, left_last = corner[0, b], corner[1, b]
        right_first, right_last = corner[2, b], corner[3, b]
        gain = 1.0 / (1.0 - left_first * reach)
        carry_ref[0, b] = left_last * gain
        carry_ref[1, b] = left_last * reach * gain
        carry_ref[2, b] = gain
        carry_ref[3, b] = gain * left_first
        carry_ref[4, b] = gain * right_first
        carry_ref[5, b] = reach
        reach = right_last + left_last * reach * gain * right_first

    start = block * rows
    low, up = low_ref[start], up_ref[start]
    inverse = 1.0 / (low + up + shift)
    ratio_ref[0] = jnp.zeros_like(shift)
    inverse_ref[0] = inverse
    back_ref[0] = up * inverse
    chain = low * jnp.ones_like(shift)
    left_ref[0] = chain

    def own_forward(j, state):
        inverse, chain = state
        low, up, before = low_ref[start + j], up_ref[start + j], up_ref[start + j - 1]
        ratio = low * inverse
        inverse = 1.0 / (low + up + shift - ratio * before)
        chain = chain * ratio
        ratio_ref[j] = ratio
        inverse_ref[j] = inverse
        back_ref[j] = up * inverse
        left_ref[j] = chain
        return (inverse, chain)

    lax.fori_loop(1, rows, own_forward, (inverse, chain))

    def own_backward(i, state):
        left, right = state
        j = rows - 1 - i
        back = back_ref[j]
        left = left_ref[j] * inverse_ref[j] + back * left
        right = back * right
        left_ref[j] = left
        right_ref[j] = right
        return (left, right)

    lax.fori_loop(
        0, rows, own_backward, (jnp.zeros_like(shift), jnp.ones_like(shift)), unroll=4
    )


def sweep_kernel(
    core_ref, kept_ref, got_ref, ratio_ref, inverse_ref, back_ref, solved_ref, ends_ref
):
    del core_ref
    for k in range(8):
        if k < 4:
            piece = kept_ref[0, pl.ds(128 * k, 128), :]
        else:
            piece = got_ref[pl.ds(128 * (k - 4), 128), :]
        solved_ref[pl.ds(k, 128, stride=8), :] = piece.T

    def forward(j, value):
        at = pl.ds(pl.multiple_of(j * 8, 8), 8)
        value = solved_ref[at, :] + ratio_ref[j] * value
        solved_ref[at, :] = value
        return value

    zero = jnp.zeros((8, 128), F32)
    lax.fori_loop(0, 128, forward, zero, unroll=16)

    def backward(i, value):
        j = 127 - i
        at = pl.ds(pl.multiple_of(j * 8, 8), 8)
        value = solved_ref[at, :] * inverse_ref[j] + back_ref[j] * value
        solved_ref[at, :] = value
        return value

    ends_ref[0] = lax.fori_loop(0, 128, backward, zero, unroll=16)
    ends_ref[1] = solved_ref[pl.ds(127 * 8, 8), :]


def combine_kernel(
    info_ref, ends_ref, carry_ref, solved_ref, left_ref, right_ref, out_ref, total, sums, firsts
):
    core = info_ref[0]
    block = info_ref[1]
    blocks = ends_ref.shape[0]
    before = jnp.zeros((8, 128), F32)
    for b in range(blocks):
        sums[b] = before
        first, last = ends_ref[b, 0], ends_ref[b, 1]
        before = last + carry_ref[1, b] * first + carry_ref[0, b] * before
    after = jnp.zeros((8, 128), F32)
    for b in reversed(range(blocks)):
        firsts[b + 1] = after
        base = carry_ref[2, b] * ends_ref[b, 0] + carry_ref[3, b] * sums[b]
        after = base + carry_ref[4, b] * after
    firsts[0] = after
    from_left = sums[block] + carry_ref[5, block] * firsts[block]
    from_right = firsts[block + 1]

    def join(j, unused):
        at = pl.ds(pl.multiple_of(j * 8, 8), 8)
        total[at, :] = solved_ref[at, :] + from_left * left_ref[j] + from_right * right_ref[j]
        return unused

    lax.fori_loop(0, 128, join, 0, unroll=16)
    for k in range(8):
        piece = total[pl.ds(k, 128, stride=8), :].T
        half = core if k < 4 else 1 - core
        for z in range(4):
            for part in range(2):
                rows = piece[z * 32 + part * 16 : z * 32 + part * 16 + 16]
                out_ref[part, 16 * half + 4 * (k % 4) + z] = rows


def local(source, stretch_index, mode_index):
    gx_count = lax.axis_size("gx")
    gy_count = lax.axis_size("gy")
    planes, stream_rows, wall_rows = source.shape
    length = stream_rows * gx_count
    gx_index = lax.axis_index("gx")
    gy_index = lax.axis_index("gy")
    core = gx_index % 2
    half_planes = planes // 2
    partner = [(i, i ^ 1) for i in range(gx_count)]
    chips = gx_count // 2

    core_info = core.astype(jnp.int32)[None]
    info = jnp.stack([core, gy_index]).astype(jnp.int32)

    sent = lax.dynamic_slice_in_dim(source, (1 - core) * half_planes, half_planes)
    got = lax.ppermute(sent, "gx", partner)

    starts = jnp.stack([gx_index * stream_rows, (gx_index ^ 1) * stream_rows]).astype(jnp.int32)
    table_shape = jax.ShapeDtypeStruct((gx_count, 2, 16, 256), BF16)
    table_high, table_low = pl.pallas_call(
        functools.partial(table_kernel, length),
        out_shape=(table_shape, table_shape),
        in_specs=[SMEM, VMEM],
        out_specs=(VMEM, VMEM),
        compiler_params=PARAMS,
        name="tables",
    )(starts, mode_index[:, None])
    table_high = table_high.reshape(gx_count * 32, 256)
    table_low = table_low.reshape(gx_count * 32, 256)

    table_spec = pl.BlockSpec((gx_count * 32, 256), lambda i, c: (0, 0))
    partial_sums = pl.pallas_call(
        spectrum_kernel,
        out_shape=jax.ShapeDtypeStruct((chips, 2, half_planes, 32, wall_rows), F32),
        grid_spec=pltpu.PrefetchScalarGridSpec(
            num_scalar_prefetch=1,
            grid=(half_planes // 2,),
            in_specs=[
                table_spec,
                table_spec,
                pl.BlockSpec(
                    (2, stream_rows, wall_rows), lambda i, c: (c[0] * (half_planes // 2) + i, 0, 0)
                ),
                pl.BlockSpec((2, stream_rows, wall_rows), lambda i, c: (i, 0, 0)),
            ],
            out_specs=pl.BlockSpec((chips, 2, 2, 32, wall_rows), lambda i, c: (0, 0, i, 0, 0)),
        ),
        compiler_params=PARAMS,
        name="spectrum",
    )(core_info, table_high, table_low, source, got)

    rings = [[2 * chip + c for chip in range(chips)] for c in range(2)]
    partial_sums = partial_sums.reshape(chips * half_planes * 64, wall_rows)
    summed = lax.psum_scatter(
        partial_sums, "gx", scatter_dimension=0, axis_index_groups=rings, tiled=True
    ).reshape(2, half_planes * 32, wall_rows)

    lower_all, upper_all = spacing_bands(stretch_index)
    own_modes = lax.dynamic_slice_in_dim(mode_index, gx_index * 16, 16)
    own_modes = jnp.tile(own_modes, 8)[None, :]
    column = jax.ShapeDtypeStruct((wall_rows, 8, 128), F32)
    carry_shape = jax.ShapeDtypeStruct((6, gy_count, 8, 128), F32)
    ratio, inverse, back, left, right, carry = pl.pallas_call(
        factor_kernel,
        out_shape=(column,) * 5 + (carry_shape,),
        in_specs=[SMEM, SMEM, SMEM, VMEM],
        out_specs=(VMEM,) * 6,
        scratch_shapes=[pltpu.VMEM((4, gy_count, 8, 128), F32)],
        compiler_params=PARAMS,
        name="factors",
    )(info, lower_all, upper_all, own_modes)

    given = lax.dynamic_slice_in_dim(summed, 1 - core, 1)[0]
    taken = lax.ppermute(given, "gx", partner)

    whole = pl.BlockSpec((wall_rows, 8, 128), lambda i, c: (0, 0, 0))
    solved, ends = pl.pallas_call(
        sweep_kernel,
        out_shape=(
            jax.ShapeDtypeStruct((wall_rows * 8, 128), F32),
            jax.ShapeDtypeStruct((2, 8, 128), F32),
        ),
        grid_spec=pltpu.PrefetchScalarGridSpec(
            num_scalar_prefetch=1,
            grid=(1,),
            in_specs=[
                pl.BlockSpec((1, half_planes * 32, wall_rows), lambda i, c: (c[0], 0, 0)),
                pl.BlockSpec((half_planes * 32, wall_rows), lambda i, c: (0, 0)),
                whole,
                whole,
                whole,
            ],
            out_specs=(
                pl.BlockSpec((wall_rows * 8, 128), lambda i, c: (0, 0)),
                pl.BlockSpec((2, 8, 128), lambda i, c: (0, 0, 0)),
            ),
        ),
        compiler_params=PARAMS,
        name="sweeps",
    )(core_info, summed, taken, ratio, inverse, back)

    copies = jnp.broadcast_to(ends[None], (gy_count, 2, 8, 128))
    all_ends = lax.all_to_all(copies, "gy", split_axis=0, concat_axis=0, tiled=True)

    return pl.pallas_call(
        combine_kernel,
        out_shape=jax.ShapeDtypeStruct((2, planes, 16, wall_rows), F32),
        in_specs=[SMEM] + [VMEM] * 5,
        out_specs=VMEM,
        scratch_shapes=[
            pltpu.VMEM((wall_rows * 8, 128), F32),
            pltpu.VMEM((gy_count, 8, 128), F32),
            pltpu.VMEM((gy_count + 1, 8, 128), F32),
        ],
        compiler_params=PARAMS,
        name="combine",
    )(info, all_ends, carry, solved, left, right)


def solution(mesh):
    in_specs = (P(None, "gx", "gy"), P(), P())
    out_specs = P(None, None, "gx", "gy")
    return jax.shard_map(local, mesh=mesh, in_specs=in_specs, out_specs=out_specs, check_vma=False)
```

time: 330 us -> 171 us (0.52)
  matrix products: 83 us -> 0 us
  starting transfers between devices: 60.2 us -> 3.83 us
  Pallas kernels: 0 us -> 22.5 us
  waiting for transfers between devices: 131 us -> 110 us
  other arithmetic: 17.7 us -> 0.32 us
  loops' own time: 16.6 us -> 0 us
  blocking collectives: 0 us -> 12.7 us
  between operations: 2.32 us -> 13.5 us
  local copies, waits for them, and re-layouts: 15.5 us -> 5.44 us
    all_to_all x2 -> x0, waiting for transfers between devices: 117 us -> none  [the longest x1 93.2 us: local(): lax.all_to_all(source, 'gx', split_axis=0, concat_axis=1, tiled=True)]
    reduce_scatter x0 -> x1, waiting for transfers between devices: none -> 110 us  [local(): lax.psum_scatter(partial_sums, 'gx', scatter_dimension=0, axis_index_grou...]
    dot_general x4 -> x0, matrix products: 83 us -> none  [the longest x2 41.9 us: per_block(): jnp.einsum('kx,zxy->zky', cosine_table, pencils, precision=lax.Precision....]
    ppermute x10 -> x2, starting transfers between devices: 39.8 us -> 3.83 us  [the longest x1 1.92 us: local(): taken = lax.ppermute(given, 'gx', partner)]
    pallas_call x0 -> x5, Pallas kernels: none -> 22.5 us  [the longest x1 10.7 us: local(): pl.pallas_call(factor_kernel, out_shape=(column,) * 5 + (carry_shape,), i...]
    all_to_all x2 -> x0, starting transfers between devices: 20.4 us -> none  [the longest x1 15.7 us: local(): lax.all_to_all(source, 'gx', split_axis=0, concat_axis=1, tiled=True)]
    another operation x1 -> x0, loops' own time: 16.6 us -> none  [transform(): stacked = lax.map(per_block, groups)]
    ppermute x10 -> x2, waiting for transfers between devices: 14.1 us -> 0.31 us  [the longest x1 0.31 us: local(): got = lax.ppermute(sent, 'gx', partner)]
  transfers between devices with their start and end apart: 12 -> 3, of which waited for: 8 -> 2; matrix products, arithmetic and copies ran while one was open for 5% -> 0% of each run, Pallas kernels for 0% -> 8%
where the time goes in v1:
time: 171 us; the launch traced here: 168 us
  waiting for transfers between devices  110 us (64%)
  Pallas kernels  22.5 us (13%)
  between operations  13.5 us (8%)
  blocking collectives  12.7 us (7%)
  local copies, waits for them, and re-layouts  5.44 us (3%)
  starting transfers between devices  3.83 us (2%)
    reduce_scatter x1, waiting for transfers between devices, local(): lax.psum_scatter(partial_sums, 'gx', scatter_dimension=0, axis_index_grou...  110 us
    all_to_all x1, blocking collectives, local(): lax.all_to_all(copies, 'gy', split_axis=0, concat_axis=0, tiled=True)  12.7 us
    pallas_call x1, Pallas kernels, local(): pl.pallas_call(factor_kernel, out_shape=(column,) * 5 + (carry_shape,), i...  10.7 us
    pallas_call x1, Pallas kernels, local(): pl.pallas_call(spectrum_kernel, out_shape=jax.ShapeDtypeStruct((chips, 2,...  6.75 us
  transfers between devices with their start and end apart: 3, of which 2 were waited for; matrix products, arithmetic and copies ran while one was open for 0% of the time, Pallas kernels for 8%

profile of v1, /device:TPU:24, one launch (start us, length us, event | category | flops | bytes accessed | tf_op | source)
XLA Modules:
  0.0 168.4 jit_solution(8483486198871391015)
XLA Ops:
  6.5 0.0 copy-start
  6.5 0.0 copy-start.3
  6.5 0.0 reduce-scatter.2.cloned.1.call-start
  6.5 2.5 %constant_dynamic-slice_fusion = f32[16,128,128]{2,1,0:T(8,128)} fusion(f32[32,128,128]{2,1,0:T(8,128)} %own_ref.1, s32[]{:T(128)S(6)} %select_n.17), kind=kLoop, calls=%fused_computation.9 | loop fusion | bytes 2097156 | tf_op jit(solution)/shard_map/dynamic_slice | solution.py:274
  9.0 1.9 %collective-permute-start = (f32[16,128,128]{2,1,0:T(8,128)}, f32[16,128,128]{2,1,0:T(8,128)S(1)}, u32[]{:S(2)}, u32[]{:S(2)}) collective-permute-start(f32[16,128,128]{2,1,0:T(8,128)} %constant_dynamic-slice_fusion), channel_id=1, source_target_pairs={{0,16},{16,0},{32,48},{48,32},{64,80},{80,64},{96,112},{112,96},{1... | collective-permute-start | bytes 3145736 | tf_op jit(solution)/shard_map/ppermute | solution.py:275
  10.9 0.0 copy-done.3
  10.9 0.1 copy.4.modes_ref
  11.1 0.1 pad_add_fusion.1.starts_ref
  11.2 2.3 %tables.1 = (bf16[32,2,16,256]{3,2,1,0:T(8,128)(2,1)S(1)}, bf16[32,2,16,256]{3,2,1,0:T(8,128)(2,1)S(1)}) custom-call(s32[2]{0:T(128)S(1)} %pad_add_fusion.1.starts_ref, s32[512,1]{1,0:T(8,128)S(1)} %copy.4.modes_ref), custom_call_target="tpu_custom_call" | custom-call | tf_op jit(solution)/shard_map/tables/pallas_call | solution.py:279
  13.4 0.3 collective-permute-done.got_ref
  13.7 0.0 copy-done
  13.8 6.8 %spectrum.1 = f32[16,2,16,32,128]{4,3,2,1,0:T(8,128)} custom-call(s32[1]{0:T(128)} %bitcast.core_ref, bf16[1024,256]{1,0:T(8,128)(2,1)S(1)} %bitcast.13, bf16[1024,256]{1,0:T(8,128)(2,1)S(1)} %bitcast.14, f32[32,128,128]{2,1,0:T(8,128)S(1)} %copy-done, f32[16,128,128]{2,1,0:T(8,128)S(1)} %collective-permute-done.got_ref), custom_call_target="tpu_custom_call" | custom-call | tf_op jit(solution)/shard_map/spectrum/pallas_call | solution.py:291
  20.5 0.0 copy-start.2
  20.5 0.0 reduce-scatter.2.cloned.1.call-update
  20.5 0.7 copy-done.2
  21.2 109.8 %reduce-scatter.2.cloned.1.call-done = f32[1024,128]{1,0:T(8,128)} async-done(((f32[16384,128]{1,0:T(8,128)}), f32[1024,128]{1,0:T(8,128)}) %reduce-scatter.2.cloned.1.call-update) | async-done | bytes 524304 | tf_op jit(solution)/shard_map/reduce_scatter | solution.py:313
  131.0 1.0 dynamic-slice_bitcast_fusion
  131.9 1.9 %collective-permute-start.1 = (f32[512,128]{1,0:T(8,128)S(1)}, f32[512,128]{1,0:T(8,128)S(1)}, u32[]{:S(2)}, u32[]{:S(2)}) collective-permute-start(f32[512,128]{1,0:T(8,128)S(1)} %dynamic-slice_bitcast_fusion), channel_id=1, source_target_pairs={{0,16},{16,0},{32,48},{48,32},{64,80},{80,64},{96,112},{112,96},{1... | collective-permute-start | bytes 786440 | tf_op jit(solution)/shard_map/ppermute | solution.py:333
  133.9 0.1 multiply_divide_fusion
  134.0 0.1 dynamic_slice.11
  134.0 0.1 broadcast_in_dim_tile.3.modes_ref
  134.1 0.1 pad_add_fusion.info_ref
  134.2 0.1 pad_maximum_fusion
  134.3 10.7 %factors.1 = (f32[128,8,128]{2,1,0:T(8,128)S(1)}, f32[128,8,128]{2,1,0:T(8,128)S(1)}, f32[128,8,128]{2,1,0:T(8,128)S(1)}, f32[128,8,128]{2,1,0:T(8,128)S(1)}, f3...) custom-call(s32[2]{0:T(128)S(1)} %pad_add_fusion.info_ref, f32[2048]{0:T(1024)S(1)} %get-tuple-element.27.low_ref, ...), custom_call_target="tpu_custom_call" | custom-call | tf_op jit(solution)/shard_map/factors/pallas_call | solution.py:322
  145.0 0.0 collective-permute-done.1.got_ref
  145.0 0.0 copy-start.1
  145.0 1.0 copy-done.1
  146.0 1.0 sweeps.1
  147.1 12.7 %all_to_all.5.ends_ref = f32[16,2,8,128]{3,2,1,0:T(8,128)S(1)} all-to-all(f32[16,2,8,128]{3,2,1,0:T(8,128)S(1)} %broadcast_in_dim.5), channel_id=1, replica_groups=mesh['gx'=32,'gy'=16] {'gy'}, dimensions={0} | all-to-all | bytes 262144 | tf_op jit(solution)/shard_map/all_to_all | solution.py:362
  159.8 1.7 %combine.1 = f32[2,32,16,128]{3,2,1,0:T(8,128)} custom-call(s32[2]{0:T(128)S(1)} %pad_add_fusion.info_ref, f32[16,2,8,128]{3,2,1,0:T(8,128)S(1)} %all_to_all.5.ends_ref, f32[6,16,8,128]{3,2,1,0:T(8,128)S(1)} %get-tuple-element.21.carry_ref, f32[1024,128]{1,0:T(8,128)S(1)} %get-tuple-element.22.solved_ref, f32[128,8,128]{2,1,0:T(8,128)S(1)} %get-tuple-element.23.left_ref, ...), custom_call_target="tpu_custom_call" | custom-call | tf_op jit(solution)/shard_map/combine/pallas_call | solution.py:364
  (3 shorter events, 0.0 us)
Async XLA Ops:
  6.5 7.2 %copy-start = (f32[32,128,128]{2,1,0:T(8,128)S(1)}, f32[32,128,128]{2,1,0:T(8,128)}, u32[]{:S(2)}) copy-start(f32[32,128,128]{2,1,0:T(8,128)} %own_ref.1) | copy-start | bytes 6291460
  6.5 4.4 %copy-start.3 = (s32[512]{0:T(512)S(1)}, s32[512]{0:T(512)}, u32[]{:S(2)}) copy-start(s32[512]{0:T(512)} %param.5) | copy-start | bytes 6148
  6.5 124.4 %reduce-scatter.2.cloned.1.call-start = ((), (), s32[]{:S(2)}) async-start(), calls=%async_computation.2 | async-start | bytes 8912896 | tf_op jit(solution)/shard_map/reduce_scatter | solution.py:313
  9.0 4.8 %collective-permute-start = (f32[16,128,128]{2,1,0:T(8,128)}, f32[16,128,128]{2,1,0:T(8,128)S(1)}, u32[]{:S(2)}, u32[]{:S(2)}) collective-permute-start(f32[16,128,128]{2,1,0:T(8,128)} %constant_dynamic-slice_fusion), channel_id=1, source_target_pairs={{0,16},{16,0},{32,48},{48,32},{64,80},{80,64},{96,112},{112,96},{1... | collective-permute-start | bytes 3145736 | tf_op jit(solution)/shard_map/ppermute | solution.py:275
  20.5 0.7 copy-start.2
  131.9 13.0 %collective-permute-start.1 = (f32[512,128]{1,0:T(8,128)S(1)}, f32[512,128]{1,0:T(8,128)S(1)}, u32[]{:S(2)}, u32[]{:S(2)}) collective-permute-start(f32[512,128]{1,0:T(8,128)S(1)} %dynamic-slice_bitcast_fusion), channel_id=1, source_target_pairs={{0,16},{16,0},{32,48},{48,32},{64,80},{80,64},{96,112},{112,96},{1... | collective-permute-start | bytes 786440 | tf_op jit(solution)/shard_map/ppermute | solution.py:333
  145.0 1.0 copy-start.1
Sparse Core Ops, SparseCore 0:
  20.7 110.2 reduce-scatter.1

commit v2 on v1

v2 whole, which is shorter than its diff:
```python
import functools
import math

import jax
import jax.numpy as jnp
from jax import lax
from jax.experimental import pallas as pl
from jax.experimental.pallas import tpu as pltpu
from jax.sharding import PartitionSpec as P

F32 = jnp.float32
BF16 = jnp.bfloat16
VMEM = pl.BlockSpec(memory_space=pltpu.VMEM)
SMEM = pl.BlockSpec(memory_space=pltpu.SMEM)
PARAMS = pltpu.CompilerParams(vmem_limit_bytes=48 * 1024 * 1024)


def spacing_bands(stretch_index):
    spacing = 0.25 * jnp.exp2(0.25 * stretch_index.astype(F32))
    faces = 0.5 * (spacing[:-1] + spacing[1:])
    zeros_one = jnp.zeros((1,), F32)
    lower_band = jnp.concatenate([zeros_one, 1.0 / (spacing[1:] * faces)])
    upper_band = jnp.concatenate([1.0 / (spacing[:-1] * faces), zeros_one])
    return (lower_band, upper_band)


def halves(values):
    high = values.astype(BF16)
    low = (values - high.astype(F32)).astype(BF16)
    return high, low


def wave(phase, length):
    quarter = length // 4
    phase = phase & (length - 1)
    turn = (phase + quarter // 2) // quarter
    angle = (phase - turn * quarter).astype(F32) * (2.0 * math.pi / length)
    square = angle * angle
    sine = angle * (
        1.0
        + square
        * (-1.0 / 6 + square * (1.0 / 120 + square * (-1.0 / 5040 + square * (1.0 / 362880))))
    )
    cosine = 1.0 + square * (
        -0.5 + square * (1.0 / 24 + square * (-1.0 / 720 + square * (1.0 / 40320)))
    )
    odd = (turn & 1) == 1
    real = jnp.where(odd, sine, cosine)
    imag = jnp.where(odd, cosine, sine)
    real = jnp.where(((turn + 1) & 2) == 2, -real, real)
    imag = jnp.where((turn & 2) == 2, -imag, imag)
    return real, imag


def table_kernel(length, starts_ref, modes_ref, high_ref, low_ref):
    mode_column = modes_ref[...]
    for side in range(2):
        place = starts_ref[side] + lax.broadcasted_iota(jnp.int32, (1, 128), 1)
        real, imag = wave(mode_column * place, length)
        scale = 1.0 / math.sqrt(length)
        columns = pl.ds(side * 128, 128)
        for part, values in enumerate((real * scale, imag * -scale)):
            high, low = halves(values)
            high_ref[:, part, :, columns] = high.reshape(-1, 16, 128)
            low_ref[:, part, :, columns] = low.reshape(-1, 16, 128)


def spectrum_kernel(high_ref, low_ref, own_ref, got_ref, out_ref):
    count = own_ref.shape[0]
    for plane in range(0, count, 2):
        field = jnp.concatenate(
            [
                jnp.concatenate([own_ref[plane], own_ref[plane + 1]], 1),
                jnp.concatenate([got_ref[plane], got_ref[plane + 1]], 1),
            ],
            0,
        )
        field_high, field_low = halves(field)
        step = 8
        for first in range(0, out_ref.shape[0], step):
            rows = pl.ds(first * 32, step * 32)
            high = high_ref[rows, :]
            total = jnp.dot(high, field_high, preferred_element_type=F32)
            total += jnp.dot(high, field_low, preferred_element_type=F32)
            total += jnp.dot(low_ref[rows, :], field_high, preferred_element_type=F32)
            for k in range(2):
                piece = total[:, k * 128 : (k + 1) * 128]
                out_ref[pl.ds(first, step), plane + k] = piece.reshape(step, 32, 128)


def shift_of(plane, modes):
    span_wave = 0.04 * (plane.astype(F32) + 1.0)
    stream_wave = modes.astype(F32) * (2.0 * math.pi / 4096)
    return span_wave * span_wave + stream_wave * stream_wave


def carry_kernel(low_ref, up_ref, modes_ref, carry_ref, corner):
    rows = 128
    blocks = carry_ref.shape[1]
    sublane = lax.broadcasted_iota(jnp.int32, (8, 128), 0)
    lane = lax.broadcasted_iota(jnp.int32, (8, 128), 1)
    shift = shift_of(4 * sublane + lane // 32, modes_ref[...])

    group = 8
    for first in range(0, blocks, group):
        state = []
        for b in range(first, first + group):
            low, up = low_ref[b * rows], up_ref[b * rows]
            inverse = 1.0 / (low + up + shift)
            state.append((inverse, jnp.ones_like(shift), up * inverse, inverse))

        def forward(j, state):
            later = []
            for k in range(group):
                at = (first + k) * rows + j
                low, up, before = low_ref[at], up_ref[at], up_ref[at - 1]
                inverse, chain, product, corner_sum = state[k]
                ratio = low * inverse
                inverse = 1.0 / (low + up + shift - ratio * before)
                chain = chain * ratio
                corner_sum = corner_sum + product * (chain * inverse)
                later.append((inverse, chain, product * (up * inverse), corner_sum))
            return tuple(later)

        state = lax.fori_loop(1, rows, forward, tuple(state))
        for k in range(group):
            b = first + k
            inverse, chain, product, corner_sum = state[k]
            low, up = low_ref[b * rows], up_ref[b * rows + rows - 1]
            corner[0, b] = low * corner_sum
            corner[1, b] = low * (chain * inverse)
            corner[2, b] = product
            corner[3, b] = up * inverse

    reach = jnp.zeros_like(shift)
    for b in range(blocks):
        left_first, left_last = corner[0, b], corner[1, b]
        right_first, right_last = corner[2, b], corner[3, b]
        gain = 1.0 / (1.0 - left_first * reach)
        carry_ref[0, b] = left_last * gain
        carry_ref[1, b] = left_last * reach * gain
        carry_ref[2, b] = gain
        carry_ref[3, b] = gain * left_first
        carry_ref[4, b] = gain * right_first
        carry_ref[5, b] = reach
        reach = right_last + left_last * reach * gain * right_first


def weights_kernel(info_ref, low_ref, up_ref, modes_ref, first_ref, last_ref):
    rows = 128
    groups = first_ref.shape[0]
    start = info_ref[1] * rows
    end = start + rows - 1
    sublane = lax.broadcasted_iota(jnp.int32, (8, 128), 0)
    shifts = [shift_of(4 * w + sublane // 2, modes_ref[...]) for w in range(groups)]

    state = []
    for w in range(groups):
        down = 1.0 / (low_ref[start] + up_ref[start] + shifts[w])
        rising = 1.0 / (low_ref[end] + up_ref[end] + shifts[w])
        last_ref[w, pl.ds(0, 8), :] = down
        first_ref[w, pl.ds(8 * (rows - 1), 8), :] = rising
        state += [down, rising]

    def eliminate(i, state):
        j, k = start + i, end - i
        later = []
        for w in range(groups):
            down, rising = state[2 * w], state[2 * w + 1]
            down = 1.0 / (low_ref[j] + up_ref[j] + shifts[w] - (low_ref[j] * down) * up_ref[j - 1])
            last_ref[w, pl.ds(pl.multiple_of(8 * i, 8), 8), :] = down
            rising = 1.0 / (
                low_ref[k] + up_ref[k] + shifts[w] - (up_ref[k] * rising) * low_ref[k + 1]
            )
            first_ref[w, pl.ds(pl.multiple_of(8 * (rows - 1 - i), 8), 8), :] = rising
            later += [down, rising]
        return tuple(later)

    state = lax.fori_loop(1, rows, eliminate, tuple(state))

    def spread(i, state):
        j = rows - 1 - i
        later = []
        for w in range(groups):
            last, first = state[2 * w], state[2 * w + 1]
            at = pl.ds(pl.multiple_of(8 * j, 8), 8)
            last = last * (low_ref[start + j + 1] * last_ref[w, at, :])
            last_ref[w, at, :] = last
            at = pl.ds(pl.multiple_of(8 * i, 8), 8)
            first = first * (up_ref[start + i - 1] * first_ref[w, at, :])
            first_ref[w, at, :] = first
            later += [last, first]
        return tuple(later)

    lax.fori_loop(1, rows, spread, state)


def ends_kernel(sums_ref, first_ref, last_ref, ends_ref):
    for row in range(8):
        plane, half = row // 2, row % 2
        at = pl.ds(row, 128, stride=8)
        first, last = first_ref[0, at, :], last_ref[0, at, :]
        for part in range(2):
            values = sums_ref[pl.ds(8 * half, 8), plane, pl.ds(16 * part, 16), :]
            values = values.reshape(128, 128).T
            ends_ref[0, part, pl.ds(row, 1), :] = jnp.sum(values * first, 0, keepdims=True)
            ends_ref[1, part, pl.ds(row, 1), :] = jnp.sum(values * last, 0, keepdims=True)


def interface_kernel(info_ref, ends_ref, carry_ref, edge_ref, sums, firsts):
    block = info_ref[1]
    blocks = ends_ref.shape[0]
    before = jnp.zeros((8, 128), F32)
    for b in range(blocks):
        sums[b] = before
        before = ends_ref[b, 1] + carry_ref[1, b] * ends_ref[b, 0] + carry_ref[0, b] * before
    after = jnp.zeros((8, 128), F32)
    for b in reversed(range(blocks)):
        firsts[b + 1] = after
        base = carry_ref[2, b] * ends_ref[b, 0] + carry_ref[3, b] * sums[b]
        after = base + carry_ref[4, b] * after
    firsts[0] = after
    edge_ref[0] = sums[block] + carry_ref[5, block] * firsts[block]
    edge_ref[1] = firsts[block + 1]


def own_factor_kernel(info_ref, low_ref, up_ref, modes_ref, ratio_ref, inverse_ref, back_ref):
    rows = 128
    sublane = lax.broadcasted_iota(jnp.int32, (8, 128), 0)
    lane = lax.broadcasted_iota(jnp.int32, (8, 128), 1)
    shift = shift_of(4 * sublane + lane // 32, modes_ref[...])
    start = info_ref[1] * rows
    low, up = low_ref[start], up_ref[start]
    inverse = 1.0 / (low + up + shift)
    ratio_ref[0] = jnp.zeros_like(shift)
    inverse_ref[0] = inverse
    back_ref[0] = up * inverse

    def forward(j, inverse):
        low, up, before = low_ref[start + j], up_ref[start + j], up_ref[start + j - 1]
        ratio = low * inverse
        inverse = 1.0 / (low + up + shift - ratio * before)
        ratio_ref[j] = ratio
        inverse_ref[j] = inverse
        back_ref[j] = up * inverse
        return inverse

    lax.fori_loop(1, rows, forward, inverse)


def solve_kernel(
    info_ref, low_ref, up_ref, sums_ref, edge_ref, ratio_ref, inverse_ref, back_ref, out_ref, work
):
    rows = 128
    start = info_ref[1] * rows
    for k in range(8):
        work[pl.ds(k, rows, stride=8), :] = sums_ref[pl.ds(128 * k, 128), :].T
    work[pl.ds(0, 8), :] += low_ref[start] * edge_ref[0]
    work[pl.ds((rows - 1) * 8, 8), :] += up_ref[start + rows - 1] * edge_ref[1]

    def forward(j, value):
        at = pl.ds(pl.multiple_of(j * 8, 8), 8)
        value = work[at, :] + ratio_ref[j] * value
        work[at, :] = value
        return value

    zero = jnp.zeros((8, 128), F32)
    lax.fori_loop(0, rows, forward, zero, unroll=16)

    def backward(i, value):
        j = rows - 1 - i
        at = pl.ds(pl.multiple_of(j * 8, 8), 8)
        value = work[at, :] * inverse_ref[j] + back_ref[j] * value
        work[at, :] = value
        return value

    lax.fori_loop(0, rows, backward, zero, unroll=16)
    for k in range(8):
        piece = work[pl.ds(k, rows, stride=8), :].T
        for z in range(4):
            for part in range(2):
                at = z * 32 + part * 16
                out_ref[part, 4 * k + z] = piece[at : at + 16]


def local(source, stretch_index, mode_index):
    gx_count = lax.axis_size("gx")
    gy_count = lax.axis_size("gy")
    planes, stream_rows, wall_rows = source.shape
    length = stream_rows * gx_count
    gx_index = lax.axis_index("gx")
    gy_index = lax.axis_index("gy")
    core = gx_index % 2
    chips = gx_count // 2
    info = jnp.stack([core, gy_index]).astype(jnp.int32)

    got = lax.ppermute(source, "gx", [(i, i ^ 1) for i in range(gx_count)])
    core_modes = lax.dynamic_slice_in_dim(mode_index.reshape(chips, 2, 16), core, 1, 1)
    core_modes = core_modes.reshape(chips * 16)

    starts = jnp.stack([gx_index * stream_rows, (gx_index ^ 1) * stream_rows]).astype(jnp.int32)
    table_shape = jax.ShapeDtypeStruct((chips, 2, 16, 256), BF16)
    table_high, table_low = pl.pallas_call(
        functools.partial(table_kernel, length),
        out_shape=(table_shape, table_shape),
        in_specs=[SMEM, VMEM],
        out_specs=(VMEM, VMEM),
        compiler_params=PARAMS,
        name="tables",
    )(starts, core_modes[:, None])

    some = 4
    table_spec = pl.BlockSpec((chips * 32, 256), lambda i: (0, 0))
    field_spec = pl.BlockSpec((some, stream_rows, wall_rows), lambda i: (i, 0, 0))
    partial_spec = pl.BlockSpec((chips, some, 32, wall_rows), lambda i: (0, i, 0, 0))
    partial_sums = pl.pallas_call(
        spectrum_kernel,
        out_shape=jax.ShapeDtypeStruct((chips, planes, 32, wall_rows), F32),
        grid=(planes // some,),
        in_specs=[table_spec, table_spec, field_spec, field_spec],
        out_specs=partial_spec,
        compiler_params=PARAMS,
        name="spectrum",
    )(
        table_high.reshape(chips * 32, 256),
        table_low.reshape(chips * 32, 256),
        source,
        got,
    )

    rings = [[2 * chip + c for chip in range(chips)] for c in range(2)]
    summed = lax.psum_scatter(
        partial_sums.reshape(chips * planes * 32, wall_rows),
        "gx",
        scatter_dimension=0,
        axis_index_groups=rings,
        tiled=True,
    )

    lower_all, upper_all = spacing_bands(stretch_index)
    groups = planes // 4
    weights = jax.ShapeDtypeStruct((groups, wall_rows * 8, 128), F32)
    first_row, last_row = pl.pallas_call(
        weights_kernel,
        out_shape=(weights, weights),
        in_specs=[SMEM, SMEM, SMEM, VMEM],
        out_specs=(VMEM, VMEM),
        compiler_params=PARAMS,
        name="weights",
    )(info, lower_all, upper_all, jnp.tile(core_modes.reshape(2, 128), (4, 1)))
    weight_spec = pl.BlockSpec((1, wall_rows * 8, 128), lambda i: (i, 0, 0))
    ends = pl.pallas_call(
        ends_kernel,
        out_shape=jax.ShapeDtypeStruct((2, 2, groups * 8, 128), F32),
        grid=(groups,),
        in_specs=[partial_spec, weight_spec, weight_spec],
        out_specs=pl.BlockSpec((2, 2, 8, 128), lambda i: (0, 0, i, 0)),
        compiler_params=PARAMS,
        name="ends",
    )(partial_sums, first_row, last_row)
    ends = ends.reshape(2, 2, planes, 2, 8, 16).transpose(3, 4, 0, 2, 1, 5)
    ends = ends.reshape(chips, 2, 8, 128)
    ends = lax.all_to_all(
        ends, "gx", split_axis=0, concat_axis=0, axis_index_groups=rings, tiled=True
    ).sum(0)
    copies = jnp.broadcast_to(ends[None], (gy_count, 2, 8, 128))
    all_ends = lax.all_to_all(copies, "gy", split_axis=0, concat_axis=0, tiled=True)

    own_modes = lax.dynamic_slice_in_dim(mode_index, gx_index * 16, 16)
    own_modes = jnp.tile(own_modes, 8)[None, :]
    carry = pl.pallas_call(
        carry_kernel,
        out_shape=jax.ShapeDtypeStruct((6, gy_count, 8, 128), F32),
        in_specs=[SMEM, SMEM, VMEM],
        out_specs=VMEM,
        scratch_shapes=[pltpu.VMEM((4, gy_count, 8, 128), F32)],
        compiler_params=PARAMS,
        name="carry",
    )(lower_all, upper_all, own_modes)
    edges = pl.pallas_call(
        interface_kernel,
        out_shape=jax.ShapeDtypeStruct((2, 8, 128), F32),
        in_specs=[SMEM, VMEM, VMEM],
        out_specs=VMEM,
        scratch_shapes=[
            pltpu.VMEM((gy_count, 8, 128), F32),
            pltpu.VMEM((gy_count + 1, 8, 128), F32),
        ],
        compiler_params=PARAMS,
        name="interfaces",
    )(info, all_ends, carry)

    column = jax.ShapeDtypeStruct((wall_rows, 8, 128), F32)
    ratio, inverse, back = pl.pallas_call(
        own_factor_kernel,
        out_shape=(column,) * 3,
        in_specs=[SMEM, SMEM, SMEM, VMEM],
        out_specs=(VMEM,) * 3,
        compiler_params=PARAMS,
        name="own_factors",
    )(info, lower_all, upper_all, own_modes)

    summed, edges, ratio = lax.optimization_barrier((summed, edges, ratio))
    return pl.pallas_call(
        solve_kernel,
        out_shape=jax.ShapeDtypeStruct((2, planes, 16, wall_rows), F32),
        in_specs=[SMEM] * 3 + [VMEM] * 5,
        out_specs=VMEM,
        scratch_shapes=[pltpu.VMEM((wall_rows * 8, 128), F32)],
        compiler_params=PARAMS,
        name="solve",
    )(info, lower_all, upper_all, summed, edges, ratio, inverse, back)


def solution(mesh):
    in_specs = (P(None, "gx", "gy"), P(), P())
    out_specs = P(None, None, "gx", "gy")
    return jax.shard_map(local, mesh=mesh, in_specs=in_specs, out_specs=out_specs, check_vma=False)
```

time: 171 us -> 150 us (0.88)
  waiting for transfers between devices: 110 us -> 44.3 us
  blocking collectives: 12.7 us -> 31.3 us
  Pallas kernels: 22.5 us -> 40.4 us
  starting transfers between devices: 3.83 us -> 9.1 us
  local copies, waits for them, and re-layouts: 5.44 us -> 9.2 us
    reduce_scatter x1, waiting for transfers between devices: 110 us -> 43.5 us  [local(): lax.psum_scatter(partial_sums.reshape(chips * planes * 32, wall_rows), 'g...]
    pallas_call x4 -> x7, Pallas kernels: 20.2 us -> 39 us  [the longest x1 9.7 us: local(): pl.pallas_call(weights_kernel, out_shape=(weights, weights), in_specs=[SM...]
    all_to_all x1, blocking collectives: 12.7 us -> 31.3 us  [local(): lax.all_to_all(ends, 'gx', split_axis=0, concat_axis=0, axis_index_groups...]
    all_to_all x0 -> x1, starting transfers between devices: none -> 7.18 us  [local(): lax.all_to_all(copies, 'gy', split_axis=0, concat_axis=0, tiled=True)]
    reshape x0 -> x3, local copies, waits for them, and re-layouts: none -> 2.37 us  [the longest x1 1.29 us: local(): ends = ends.reshape(chips, 2, 8, 128)]
    ppermute x2 -> x1, starting transfers between devices: 3.83 us -> 1.91 us  [local(): got = lax.ppermute(source, 'gx', [(i, i ^ 1) for i in range(gx_count)])]
  transfers between devices with their start and end apart: 3 -> 3, of which waited for: 2 -> 2; matrix products, arithmetic and copies ran while one was open for 0% -> 4% of each run, Pallas kernels for 8% -> 21%
where the time goes in v2:
time: 150 us; the launch traced here: 148 us
  waiting for transfers between devices  44.3 us (30%)
  Pallas kernels  40.4 us (27%)
  blocking collectives  31.3 us (21%)
  between operations  13.5 us (9%)
  local copies, waits for them, and re-layouts  9.2 us (6%)
  starting transfers between devices  9.1 us (6%)
    reduce_scatter x1, waiting for transfers between devices, local(): lax.psum_scatter(partial_sums.reshape(chips * planes * 32, wall_rows), 'g...  43.5 us
    all_to_all x1, blocking collectives, local(): lax.all_to_all(ends, 'gx', split_axis=0, concat_axis=0, axis_index_groups...  31.3 us
    pallas_call x1, Pallas kernels, local(): pl.pallas_call(weights_kernel, out_shape=(weights, weights), in_specs=[SM...  9.7 us
    pallas_call x1, Pallas kernels, local(): pl.pallas_call(carry_kernel, out_shape=jax.ShapeDtypeStruct((6, gy_count,...  8.61 us
    pallas_call x1, Pallas kernels, local(): pl.pallas_call(ends_kernel, out_shape=jax.ShapeDtypeStruct((2, 2, groups...  8.03 us
    all_to_all x1, starting transfers between devices, local(): lax.all_to_all(copies, 'gy', split_axis=0, concat_axis=0, tiled=True)  7.18 us
    pallas_call x1, Pallas kernels, local(): pl.pallas_call(spectrum_kernel, out_shape=jax.ShapeDtypeStruct((chips, pl...  6.95 us
    unnamed x6, local copies, waits for them, and re-layouts  3.15 us
  transfers between devices with their start and end apart: 3, of which 2 were waited for; matrix products, arithmetic and copies ran while one was open for 4% of the time, Pallas kernels for 21%

profile of v2, /device:TPU:24, one launch (start us, length us, event | category | flops | bytes accessed | tf_op | source)
XLA Modules:
  0.0 148.1 jit_solution(3372330672133221302)
XLA Ops:
  6.5 0.0 reduce-scatter.2.cloned.1.call-start
  6.5 1.9 %collective-permute-start = (f32[32,128,128]{2,1,0:T(8,128)}, f32[32,128,128]{2,1,0:T(8,128)S(1)}, u32[]{:S(2)}, u32[]{:S(2)}) collective-permute-start(f32[32,128,128]{2,1,0:T(8,128)} %own_ref.1), channel_id=1, source_target_pairs={{0,16},{16,0},{32,48},{48,32},{64,80},{80,64},{96,112},{112,96},{1... | collective-permute-start | bytes 6291464 | tf_op jit(solution)/shard_map/ppermute | solution.py:297
  8.5 0.8 reshape.24
  9.3 0.5 broadcast.22
  9.8 0.7 fusion
  10.4 0.1 broadcast_in_dim_reshape.4.modes_ref
  10.6 0.1 pad_add_fusion.1.starts_ref
  10.6 1.4 tables.1
  12.0 0.8 collective-permute-done.got_ref
  12.8 0.0 copy-start
  12.8 1.6 %copy-done = f32[32,128,128]{2,1,0:T(8,128)S(1)} copy-done((f32[32,128,128]{2,1,0:T(8,128)S(1)}, f32[32,128,128]{2,1,0:T(8,128)}, u32[]{:S(2)}) %copy-start) | copy-done | bytes 2097176
  14.4 7.0 %spectrum.1.sums_ref = f32[16,32,32,128]{3,2,1,0:T(8,128)} custom-call(bf16[512,256]{1,0:T(8,128)(2,1)S(1)} %bitcast.12, bf16[512,256]{1,0:T(8,128)(2,1)S(1)} %bitcast.13, f32[32,128,128]{2,1,0:T(8,128)S(1)} %copy-done, f32[32,128,128]{2,1,0:T(8,128)S(1)} %collective-permute-done.got_ref), custom_call_target="tpu_custom_call" | custom-call | tf_op jit(solution)/shard_map/spectrum/pallas_call | solution.py:316
  21.3 0.0 copy-start.2
  21.3 0.0 reduce-scatter.2.cloned.1.call-update
  21.4 0.1 tile.16
  21.4 0.1 pad_add_fusion.info_ref
  21.5 0.5 copy-done.2
  22.0 0.1 multiply_divide_fusion
  22.1 0.1 pad_maximum_fusion
  22.2 9.7 %weights.1 = (f32[8,1024,128]{2,1,0:T(8,128)S(1)}, f32[8,1024,128]{2,1,0:T(8,128)}) custom-call(s32[2]{0:T(128)S(1)} %pad_add_fusion.info_ref, f32[2048]{0:T(1024)S(1)} %get-tuple-element.29.low_ref, f32[2048]{0:T(1024)S(1)} %get-tuple-element.30.up_ref, s32[8,128]{1,0:T(8,128)S(1)} %bitcast.14), custom_call_target="tpu_custom_call" | custom-call | tf_op jit(solution)/shard_map/weights/pallas_call | solution.py:343
  31.9 8.0 %ends.1 = f32[2,2,64,128]{3,2,1,0:T(8,128)S(1)} custom-call(f32[16,32,32,128]{3,2,1,0:T(8,128)} %spectrum.1.sums_ref, f32[8,1024,128]{2,1,0:T(8,128)S(1)} %get-tuple-element.17.first_ref, f32[8,1024,128]{2,1,0:T(8,128)} %get-tuple-element.18.last_ref), custom_call_target="tpu_custom_call" | custom-call | tf_op jit(solution)/shard_map/ends/pallas_call | solution.py:352
  39.9 0.3 reshape.28
  40.3 0.8 copy.5
  41.1 1.3 reshape.29
  42.4 31.3 %all_to_all.10 = f32[16,2,8,128]{3,2,1,0:T(8,128)S(1)} all-to-all(f32[16,2,8,128]{3,2,1,0:T(8,128)S(1)} %reshape.29), channel_id=1, replica_groups={{0,32,64,96,128,160,192,224,256,288,320,352,384,416,448,480},{16,48,80,..., dimensions={0} | all-to-all | bytes 262144 | tf_op jit(solution)/shard_map/all_to_all | solution.py:363
  73.7 0.7 broadcast_in_dim.2
  74.3 7.2 %all-to-all-start.1 = ((f32[16,2,8,128]{3,2,1,0:T(8,128)}), f32[16,2,8,128]{3,2,1,0:T(8,128)S(1)}, u32[]{:S(2)}, u32[]{:S(2)}) async-start(f32[16,2,8,128]{3,2,1,0:T(8,128)} %broadcast_in_dim.2), calls=%async_computation.2 | async-start | bytes 262144 | tf_op jit(solution)/shard_map/all_to_all | solution.py:367
  81.5 0.8 dynamic_slice.7
  82.3 0.1 broadcast_in_dim_tile.3.modes_ref
  82.4 8.6 %carry.1.carry_ref = f32[6,16,8,128]{3,2,1,0:T(8,128)S(1)} custom-call(f32[2048]{0:T(1024)S(1)} %get-tuple-element.29.low_ref, f32[2048]{0:T(1024)S(1)} %get-tuple-element.30.up_ref, s32[1,128]{1,0:T(1,128)S(1)} %broadcast_in_dim_tile.3.modes_ref), custom_call_target="tpu_custom_call" | custom-call | tf_op jit(solution)/shard_map/carry/pallas_call | solution.py:371
  91.0 2.3 %own_factors.1 = (f32[128,8,128]{2,1,0:T(8,128)S(1)}, f32[128,8,128]{2,1,0:T(8,128)S(1)}, f32[128,8,128]{2,1,0:T(8,128)S(1)}) custom-call(s32[2]{0:T(128)S(1)} %pad_add_fusion.info_ref, f32[2048]{0:T(1024)S(1)} %get-tuple-element.29.low_ref, f32[2048]{0:T(1024)S(1)} %get-tuple-element.30.up_ref, s32[1,128]{1,0:T(1,128)S(1)} %broadcast_in_dim_tile.3.modes_ref), custom_call_target="tpu_custom_call" | custom-call | tf_op jit(solution)/shard_map/own_factors/pallas_call | solution.py:394
  93.3 0.0 all-to-all-done.1.ends_ref
  93.3 0.6 interfaces.1.edge_ref
  93.9 43.5 %reduce-scatter.2.cloned.1.call-done.sums_ref = f32[1024,128]{1,0:T(8,128)} async-done(((f32[16384,128]{1,0:T(8,128)}), f32[1024,128]{1,0:T(8,128)}) %reduce-scatter.2.cloned.1.call-update) | async-done | bytes 524304 | tf_op jit(solution)/shard_map/reduce_scatter | solution.py:332
  137.4 0.0 copy-start.1
  137.4 1.0 copy-done.1
  138.5 2.8 %solve.1 = f32[2,32,16,128]{3,2,1,0:T(8,128)} custom-call(s32[2]{0:T(128)S(1)} %pad_add_fusion.info_ref, f32[2048]{0:T(1024)S(1)} %get-tuple-element.29.low_ref, f32[2048]{0:T(1024)S(1)} %get-tuple-element.30.up_ref, f32[1024,128]{1,0:T(8,128)S(1)} %copy-done.1, f32[2,8,128]{2,1,0:T(8,128)S(1)} %interfaces.1.edge_ref, ...), custom_call_target="tpu_custom_call" | custom-call | tf_op jit(solution)/shard_map/solve/pallas_call | solution.py:404
  (4 shorter events, 0.0 us)
Async XLA Ops:
  6.5 130.9 %reduce-scatter.2.cloned.1.call-start = ((), (), s32[]{:S(2)}) async-start(), calls=%async_computation.3 | async-start | bytes 8912896 | tf_op jit(solution)/shard_map/reduce_scatter | solution.py:332
  6.5 6.3 %collective-permute-start = (f32[32,128,128]{2,1,0:T(8,128)}, f32[32,128,128]{2,1,0:T(8,128)S(1)}, u32[]{:S(2)}, u32[]{:S(2)}) collective-permute-start(f32[32,128,128]{2,1,0:T(8,128)} %own_ref.1), channel_id=1, source_target_pairs={{0,16},{16,0},{32,48},{48,32},{64,80},{80,64},{96,112},{112,96},{1... | collective-permute-start | bytes 6291464 | tf_op jit(solution)/shard_map/ppermute | solution.py:297
  12.8 1.6 %copy-start = (f32[32,128,128]{2,1,0:T(8,128)S(1)}, f32[32,128,128]{2,1,0:T(8,128)}, u32[]{:S(2)}) copy-start(f32[32,128,128]{2,1,0:T(8,128)} %own_ref.1) | copy-start | bytes 6291460
  21.3 0.7 copy-start.2
  74.3 18.9 %all-to-all-start.1 = ((f32[16,2,8,128]{3,2,1,0:T(8,128)}), f32[16,2,8,128]{3,2,1,0:T(8,128)S(1)}, u32[]{:S(2)}, u32[]{:S(2)}) async-start(f32[16,2,8,128]{3,2,1,0:T(8,128)} %broadcast_in_dim.2), calls=%async_computation.2 | async-start | bytes 262144 | tf_op jit(solution)/shard_map/all_to_all | solution.py:367
  137.4 1.0 copy-start.1
Sparse Core Ops, SparseCore 0:
  21.5 115.9 reduce-scatter.1

commit v3 on v2

--- a/solution.py
+++ b/solution.py
@@ -52,10 +52,24 @@
     return real, imag
 
 
-def table_kernel(length, starts_ref, modes_ref, high_ref, low_ref):
-    mode_column = modes_ref[...]
+def table_kernel(
+    length, info_ref, modes_ref, own_ref, high_ref, low_ref, own_high_ref, own_low_ref, own, sems
+):
+    core, index = info_ref[0], info_ref[2]
+    steps = sems.shape[0]
+    some = own_ref.shape[0] // steps
+    groups = [pl.ds(some * g, some) for g in range(steps)]
+    loads = [
+        pltpu.make_async_copy(own_ref.at[groups[g]], own.at[groups[g]], sems.at[g])
+        for g in range(steps)
+    ]
+    for load in loads:
+        load.start()
+    chips = high_ref.shape[0]
+    mode_column = jnp.concatenate([modes_ref[2 * chip + core] for chip in range(chips)], 0)
     for side in range(2):
-        place = starts_ref[side] + lax.broadcasted_iota(jnp.int32, (1, 128), 1)
+        start = 128 * (index ^ side)
+        place = start + lax.broadcasted_iota(jnp.int32, (1, 128), 1)
         real, imag = wave(mode_column * place, length)
         scale = 1.0 / math.sqrt(length)
         columns = pl.ds(side * 128, 128)
@@ -63,29 +77,47 @@
             high, low = halves(values)
             high_ref[:, part, :, columns] = high.reshape(-1, 16, 128)
             low_ref[:, part, :, columns] = low.reshape(-1, 16, 128)
-
-
-def spectrum_kernel(high_ref, low_ref, own_ref, got_ref, out_ref):
-    count = own_ref.shape[0]
-    for plane in range(0, count, 2):
-        field = jnp.concatenate(
-            [
-                jnp.concatenate([own_ref[plane], own_ref[plane + 1]], 1),
-                jnp.concatenate([got_ref[plane], got_ref[plane + 1]], 1),
-            ],
-            0,
+    for g in range(steps):
+        loads[g].wait()
+        own_high_ref[groups[g]], own_low_ref[groups[g]] = halves(own[groups[g]])
+
+
+def spectrum_kernel(
+    high_ref, low_ref, own_high_ref, own_low_ref, got_ref, out_ref, sums, out_sems
+):
+    slots, chips, some = sums.shape[:3]
+    steps = got_ref.shape[0] // some
+    stores = [
+        pltpu.make_async_copy(
+            sums.at[g % slots], out_ref.at[:, pl.ds(some * g, some)], out_sems.at[g % slots]
         )
-        field_high, field_low = halves(field)
-        step = 8
-        for first in range(0, out_ref.shape[0], step):
-            rows = pl.ds(first * 32, step * 32)
-            high = high_ref[rows, :]
-            total = jnp.dot(high, field_high, preferred_element_type=F32)
-            total += jnp.dot(high, field_low, preferred_element_type=F32)
-            total += jnp.dot(low_ref[rows, :], field_high, preferred_element_type=F32)
-            for k in range(2):
-                piece = total[:, k * 128 : (k + 1) * 128]
-                out_ref[pl.ds(first, step), plane + k] = piece.reshape(step, 32, 128)
+        for g in range(steps)
+    ]
+
+    def beside(ref, plane):
+        return jnp.concatenate([ref[plane], ref[plane + 1]], 1)
+
+    for g in range(steps):
+        if g >= slots:
+            stores[g - slots].wait()
+        for pair in range(0, some, 2):
+            plane = some * g + pair
+            got_high, got_low = halves(beside(got_ref, plane))
+            field_high = jnp.concatenate([beside(own_high_ref, plane), got_high], 0)
+            field_low = jnp.concatenate([beside(own_low_ref, plane), got_low], 0)
+            step = 8
+            for first in range(0, chips, step):
+                rows = pl.ds(first * 32, step * 32)
+                high = high_ref[rows, :]
+                total = jnp.dot(high, field_high, preferred_element_type=F32)
+                total += jnp.dot(high, field_low, preferred_element_type=F32)
+                total += jnp.dot(low_ref[rows, :], field_high, preferred_element_type=F32)
+                for k in range(2):
+                    piece = total[:, k * 128 : (k + 1) * 128].reshape(step, 32, 128)
+                    sums[g % slots, pl.ds(first, step), pair + k] = piece
+        stores[g].start()
+    for g in range(max(0, steps - slots), steps):
+        stores[g].wait()
 
 
 def shift_of(plane, modes):
@@ -226,55 +258,101 @@
 
 def own_factor_kernel(info_ref, low_ref, up_ref, modes_ref, ratio_ref, inverse_ref, back_ref):
     rows = 128
+    half = rows // 2
     sublane = lax.broadcasted_iota(jnp.int32, (8, 128), 0)
     lane = lax.broadcasted_iota(jnp.int32, (8, 128), 1)
     shift = shift_of(4 * sublane + lane // 32, modes_ref[...])
     start = info_ref[1] * rows
-    low, up = low_ref[start], up_ref[start]
-    inverse = 1.0 / (low + up + shift)
+    end = start + rows - 1
+
+    def pivot(at):
+        return low_ref[at] + up_ref[at] + shift
+
+    down = 1.0 / pivot(start)
+    rising = 1.0 / pivot(end)
     ratio_ref[0] = jnp.zeros_like(shift)
-    inverse_ref[0] = inverse
-    back_ref[0] = up * inverse
-
-    def forward(j, inverse):
-        low, up, before = low_ref[start + j], up_ref[start + j], up_ref[start + j - 1]
-        ratio = low * inverse
-        inverse = 1.0 / (low + up + shift - ratio * before)
-        ratio_ref[j] = ratio
-        inverse_ref[j] = inverse
-        back_ref[j] = up * inverse
-        return inverse
-
-    lax.fori_loop(1, rows, forward, inverse)
+    ratio_ref[rows - 1] = jnp.zeros_like(shift)
+    inverse_ref[0] = down
+    inverse_ref[rows - 1] = rising
+    back_ref[0] = up_ref[start] * down
+    back_ref[rows - 1] = low_ref[end] * rising
+
+    def eliminate(i, state):
+        down, rising = state
+        j, k = start + i, end - i
+        ratio = low_ref[j] * down
+        down = 1.0 / (pivot(j) - ratio * up_ref[j - 1])
+        ratio_ref[i] = ratio
+        inverse_ref[i] = down
+        back_ref[i] = up_ref[j] * down
+        ratio = up_ref[k] * rising
+        rising = 1.0 / (pivot(k) - ratio * low_ref[k + 1])
+        ratio_ref[rows - 1 - i] = ratio
+        inverse_ref[rows - 1 - i] = rising
+        back_ref[rows - 1 - i] = low_ref[k] * rising
+        return (down, rising)
+
+    down, rising = lax.fori_loop(1, half, eliminate, (down, rising))
+    across = 1.0 / (1.0 - back_ref[half - 1] * back_ref[half])
+    inverse_ref[half - 1] = down * across
+    inverse_ref[half] = rising * across
 
 
 def solve_kernel(
-    info_ref, low_ref, up_ref, sums_ref, edge_ref, ratio_ref, inverse_ref, back_ref, out_ref, work
+    info_ref,
+    low_ref,
+    up_ref,
+    sums_ref,
+    edge_ref,
+    ratio_ref,
+    inverse_ref,
+    back_ref,
+    out_ref,
+    work,
 ):
     rows = 128
+    half = rows // 2
     start = info_ref[1] * rows
     for k in range(8):
-        work[pl.ds(k, rows, stride=8), :] = sums_ref[pl.ds(128 * k, 128), :].T
-    work[pl.ds(0, 8), :] += low_ref[start] * edge_ref[0]
-    work[pl.ds((rows - 1) * 8, 8), :] += up_ref[start + rows - 1] * edge_ref[1]
-
-    def forward(j, value):
-        at = pl.ds(pl.multiple_of(j * 8, 8), 8)
-        value = work[at, :] + ratio_ref[j] * value
-        work[at, :] = value
-        return value
-
-    zero = jnp.zeros((8, 128), F32)
-    lax.fori_loop(0, rows, forward, zero, unroll=16)
-
-    def backward(i, value):
-        j = rows - 1 - i
-        at = pl.ds(pl.multiple_of(j * 8, 8), 8)
-        value = work[at, :] * inverse_ref[j] + back_ref[j] * value
-        work[at, :] = value
-        return value
-
-    lax.fori_loop(0, rows, backward, zero, unroll=16)
+        work[pl.ds(k, rows, stride=8), :] = sums_ref[pl.ds(rows * k, rows), :].T
+
+    def row(j):
+        return pl.ds(pl.multiple_of(j * 8, 8), 8)
+
+    upper = work[row(0), :] + low_ref[start] * edge_ref[0]
+    lower = work[row(rows - 1), :] + up_ref[start + rows - 1] * edge_ref[1]
+    work[row(0), :] = upper
+    work[row(rows - 1), :] = lower
+
+    def inwards(j, state):
+        upper, lower = state
+        k = rows - 1 - j
+        upper = work[row(j), :] + ratio_ref[j] * upper
+        work[row(j), :] = upper
+        lower = work[row(k), :] + ratio_ref[k] * lower
+        work[row(k), :] = lower
+        return (upper, lower)
+
+    upper, lower = lax.fori_loop(1, half, inwards, (upper, lower), unroll=63)
+
+    first = upper * inverse_ref[half - 1]
+    second = lower * inverse_ref[half]
+    upper = first + back_ref[half - 1] * second
+    lower = second + back_ref[half] * first
+    work[row(half - 1), :] = upper
+    work[row(half), :] = lower
+
+    def outwards(i, state):
+        upper, lower = state
+        j = half - 1 - i
+        k = half + i
+        upper = work[row(j), :] * inverse_ref[j] + back_ref[j] * upper
+        work[row(j), :] = upper
+        lower = work[row(k), :] * inverse_ref[k] + back_ref[k] * lower
+        work[row(k), :] = lower
+        return (upper, lower)
+
+    lax.fori_loop(1, half, outwards, (upper, lower), unroll=63)
     for k in range(8):
         piece = work[pl.ds(k, rows, stride=8), :].T
         for z in range(4):
@@ -292,39 +370,41 @@
     gy_index = lax.axis_index("gy")
     core = gx_index % 2
     chips = gx_count // 2
-    info = jnp.stack([core, gy_index]).astype(jnp.int32)
+    info = jnp.stack([core, gy_index, gx_index]).astype(jnp.int32)
 
     got = lax.ppermute(source, "gx", [(i, i ^ 1) for i in range(gx_count)])
-    core_modes = lax.dynamic_slice_in_dim(mode_index.reshape(chips, 2, 16), core, 1, 1)
-    core_modes = core_modes.reshape(chips * 16)
-
-    starts = jnp.stack([gx_index * stream_rows, (gx_index ^ 1) * stream_rows]).astype(jnp.int32)
+    hbm = pl.BlockSpec(memory_space=pltpu.HBM)
+    source = pltpu.with_memory_space_constraint(source, pltpu.HBM)
     table_shape = jax.ShapeDtypeStruct((chips, 2, 16, 256), BF16)
-    table_high, table_low = pl.pallas_call(
+    own_shape = jax.ShapeDtypeStruct(source.shape, BF16)
+    table_high, table_low, own_high, own_low = pl.pallas_call(
         functools.partial(table_kernel, length),
-        out_shape=(table_shape, table_shape),
-        in_specs=[SMEM, VMEM],
-        out_specs=(VMEM, VMEM),
+        out_shape=(table_shape, table_shape, own_shape, own_shape),
+        in_specs=[SMEM, VMEM, hbm],
+        out_specs=(VMEM,) * 4,
+        scratch_shapes=[pltpu.VMEM(source.shape, F32), pltpu.SemaphoreType.DMA((4,))],
         compiler_params=PARAMS,
         name="tables",
-    )(starts, core_modes[:, None])
-
-    some = 4
-    table_spec = pl.BlockSpec((chips * 32, 256), lambda i: (0, 0))
-    field_spec = pl.BlockSpec((some, stream_rows, wall_rows), lambda i: (i, 0, 0))
-    partial_spec = pl.BlockSpec((chips, some, 32, wall_rows), lambda i: (0, i, 0, 0))
+    )(info, mode_index.reshape(gx_count, 16, 1), source)
+
+    some = 8
+    slots = 3
     partial_sums = pl.pallas_call(
         spectrum_kernel,
         out_shape=jax.ShapeDtypeStruct((chips, planes, 32, wall_rows), F32),
-        grid=(planes // some,),
-        in_specs=[table_spec, table_spec, field_spec, field_spec],
-        out_specs=partial_spec,
+        in_specs=[VMEM] * 5,
+        out_specs=hbm,
+        scratch_shapes=[
+            pltpu.VMEM((slots, chips, some, 32, wall_rows), F32),
+            pltpu.SemaphoreType.DMA((slots,)),
+        ],
         compiler_params=PARAMS,
         name="spectrum",
     )(
         table_high.reshape(chips * 32, 256),
         table_low.reshape(chips * 32, 256),
-        source,
+        own_high,
+        own_low,
         got,
     )
 
@@ -339,6 +419,7 @@
 
     lower_all, upper_all = spacing_bands(stretch_index)
     groups = planes // 4
+    core_modes = lax.dynamic_slice_in_dim(mode_index.reshape(chips, 2, 16), core, 1, 1)
     weights = jax.ShapeDtypeStruct((groups, wall_rows * 8, 128), F32)
     first_row, last_row = pl.pallas_call(
         weights_kernel,
@@ -353,16 +434,25 @@
         ends_kernel,
         out_shape=jax.ShapeDtypeStruct((2, 2, groups * 8, 128), F32),
         grid=(groups,),
-        in_specs=[partial_spec, weight_spec, weight_spec],
+        in_specs=[
+            pl.BlockSpec((chips, 4, 32, wall_rows), lambda i: (0, i, 0, 0)),
+            weight_spec,
+            weight_spec,
+        ],
         out_specs=pl.BlockSpec((2, 2, 8, 128), lambda i: (0, 0, i, 0)),
         compiler_params=PARAMS,
         name="ends",
     )(partial_sums, first_row, last_row)
     ends = ends.reshape(2, 2, planes, 2, 8, 16).transpose(3, 4, 0, 2, 1, 5)
     ends = ends.reshape(chips, 2, 8, 128)
-    ends = lax.all_to_all(
-        ends, "gx", split_axis=0, concat_axis=0, axis_index_groups=rings, tiled=True
-    ).sum(0)
+    ends = jnp.take(ends, jnp.arange(chips) ^ (gx_index // 2), axis=0)
+    distance = 1
+    while distance < chips:
+        pairs = ends.reshape(-1, 2, 2, 8, 128)
+        route = [(i, i ^ (2 * distance)) for i in range(gx_count)]
+        ends = pairs[:, 0] + lax.ppermute(pairs[:, 1], "gx", route)
+        distance *= 2
+    ends = ends.reshape(2, 8, 128)
     copies = jnp.broadcast_to(ends[None], (gy_count, 2, 8, 128))
     all_ends = lax.all_to_all(copies, "gy", split_axis=0, concat_axis=0, tiled=True)
 
@@ -406,10 +496,19 @@
         out_shape=jax.ShapeDtypeStruct((2, planes, 16, wall_rows), F32),
         in_specs=[SMEM] * 3 + [VMEM] * 5,
         out_specs=VMEM,
-        scratch_shapes=[pltpu.VMEM((wall_rows * 8, 128), F32)],
+        scratch_shapes=[pltpu.VMEM((planes * 32, wall_rows), F32)],
         compiler_params=PARAMS,
         name="solve",
-    )(info, lower_all, upper_all, summed, edges, ratio, inverse, back)
+    )(
+        info,
+        lower_all,
+        upper_all,
+        pltpu.with_memory_space_constraint(summed, pltpu.HBM),
+        edges,
+        ratio,
+        inverse,
+        back,
+    )
 
 
 def solution(mesh):

time: 150 us -> 140 us (0.933)
  starting transfers between devices: 9.1 us -> 42.1 us
  blocking collectives: 31.3 us -> 0 us
  waiting for transfers between devices: 44.3 us -> 39.3 us
  local copies, waits for them, and re-layouts: 9.2 us -> 5.57 us
  Pallas kernels: 40.4 us -> 38.3 us
    ppermute x0 -> x4, starting transfers between devices: none -> 32.6 us  [local(): ends = pairs[:, 0] + lax.ppermute(pairs[:, 1], 'gx', route)]
    all_to_all x1 -> x0, blocking collectives: 31.3 us -> none  [local(): lax.all_to_all(ends, 'gx', split_axis=0, concat_axis=0, axis_index_groups...]
    reduce_scatter x1, waiting for transfers between devices: 43.5 us -> 26.9 us  [local(): lax.psum_scatter(partial_sums.reshape(chips * planes * 32, wall_rows), 'g...]
    ppermute x0 -> x4, waiting for transfers between devices: none -> 11.2 us  [local(): ends = pairs[:, 0] + lax.ppermute(pairs[:, 1], 'gx', route)]
    unnamed x6 -> x4, local copies, waits for them, and re-layouts: 3.15 us -> 0.64 us
    pallas_call x1, Pallas kernels: 6.95 us -> 4.91 us  [local(): pl.pallas_call(spectrum_kernel, out_shape=jax.ShapeDtypeStruct((chips, pl...]
  transfers between devices with their start and end apart: 3 -> 7, of which waited for: 2 -> 6; matrix products, arithmetic and copies ran while one was open for 4% -> 4% of each run, Pallas kernels for 21% -> 22%
where the time goes in v3:
time: 140 us; the launch traced here: 139 us
  starting transfers between devices  42.1 us (30%)
  waiting for transfers between devices  39.3 us (28%)
  Pallas kernels  38.3 us (27%)
  between operations  13.6 us (10%)
  local copies, waits for them, and re-layouts  5.57 us (4%)
    ppermute x4, starting transfers between devices, local(): ends = pairs[:, 0] + lax.ppermute(pairs[:, 1], 'gx', route)  32.6 us
    reduce_scatter x1, waiting for transfers between devices, local(): lax.psum_scatter(partial_sums.reshape(chips * planes * 32, wall_rows), 'g...  26.9 us
    ppermute x4, waiting for transfers between devices, local(): ends = pairs[:, 0] + lax.ppermute(pairs[:, 1], 'gx', route)  11.2 us
    pallas_call x1, Pallas kernels, local(): pl.pallas_call(weights_kernel, out_shape=(weights, weights), in_specs=[SM...  9.69 us
    pallas_call x1, Pallas kernels, local(): pl.pallas_call(carry_kernel, out_shape=jax.ShapeDtypeStruct((6, gy_count,...  8.61 us
    pallas_call x1, Pallas kernels, local(): pl.pallas_call(ends_kernel, out_shape=jax.ShapeDtypeStruct((2, 2, groups...  8.05 us
    all_to_all x1, starting transfers between devices, local(): lax.all_to_all(copies, 'gy', split_axis=0, concat_axis=0, tiled=True)  7.6 us
    pallas_call x1, Pallas kernels, local(): pl.pallas_call(spectrum_kernel, out_shape=jax.ShapeDtypeStruct((chips, pl...  4.91 us
  transfers between devices with their start and end apart: 7, of which 6 were waited for; matrix products, arithmetic and copies ran while one was open for 4% of the time, Pallas kernels for 22%

profile of v3, /device:TPU:24, one launch (start us, length us, event | category | flops | bytes accessed | tf_op | source)
XLA Modules:
  0.0 139.2 jit_solution(4903675110595678942)
XLA Ops:
  6.5 0.0 reduce-scatter.2.cloned.1.call-start
  6.5 1.9 %collective-permute-start = (f32[32,128,128]{2,1,0:T(8,128)}, f32[32,128,128]{2,1,0:T(8,128)S(1)}, u32[]{:S(2)}, u32[]{:S(2)}) collective-permute-start(f32[32,128,128]{2,1,0:T(8,128)} %own_ref.1), channel_id=1, source_target_pairs={{0,16},{16,0},{32,48},{48,32},{64,80},{80,64},{96,112},{112,96},{1... | collective-permute-start | bytes 6291464 | tf_op jit(solution)/shard_map/ppermute | solution.py:375
  8.5 0.9 reshape.78.modes_ref
  9.4 0.1 pad_add_fusion.info_ref
  9.4 2.2 %tables.1 = (bf16[16,2,16,256]{3,2,1,0:T(8,128)(2,1)S(1)}, bf16[16,2,16,256]{3,2,1,0:T(8,128)(2,1)S(1)}, bf16[32,128,128]{2,1,0:T(8,128)(2,1)S(1)}, bf16[32,128,128]{2,1,0:T(8,128)(2,1)S(1)}) custom-call(s32[3]{0:T(128)S(1)} %pad_add_fusion.info_ref, s32[32,16,1]{2,1,0:T(8,128)S(1)} %reshape.78.modes_ref, f32[32,128,128]{2,1,0:T(8,128)} %own_ref.1), custom_call_target="tpu_custom_call" | custom-call | tf_op jit(solution)/shard_map/tables/pallas_call | solution.py:380
  11.6 1.2 collective-permute-done.got_ref
  12.8 4.9 %spectrum.1.sums_ref = f32[16,32,32,128]{3,2,1,0:T(8,128)} custom-call(bf16[512,256]{1,0:T(8,128)(2,1)S(1)} %bitcast.51, bf16[512,256]{1,0:T(8,128)(2,1)S(1)} %bitcast.52, bf16[32,128,128]{2,1,0:T(8,128)(2,1)S(1)} %get-tuple-element.19.own_high_ref, bf16[32,128,128]{2,1,0:T(8,128)(2,1)S(1)} %get-tuple-element.20.own_low_ref, ...), custom_call_target="tpu_custom_call" | custom-call | tf_op jit(solution)/shard_map/spectrum/pallas_call | solution.py:392
  17.7 0.0 copy-start
  17.7 0.0 copy-start.1
  17.7 0.0 reduce-scatter.2.cloned.1.call-update
  17.8 0.6 copy-done
  18.4 0.1 reshape.64
  18.5 0.1 tile.16
  18.6 0.0 copy-done.1
  18.6 0.1 multiply_divide_fusion
  18.7 0.1 pad_maximum_fusion
  18.8 9.7 %weights.1 = (f32[8,1024,128]{2,1,0:T(8,128)S(1)}, f32[8,1024,128]{2,1,0:T(8,128)}) custom-call(s32[3]{0:T(128)S(1)} %pad_add_fusion.info_ref, f32[2048]{0:T(1024)S(1)} %get-tuple-element.31.low_ref, f32[2048]{0:T(1024)S(1)} %get-tuple-element.32.up_ref, s32[8,128]{1,0:T(8,128)S(1)} %bitcast.53), custom_call_target="tpu_custom_call" | custom-call | tf_op jit(solution)/shard_map/weights/pallas_call | solution.py:424
  28.5 8.0 %ends.1 = f32[2,2,64,128]{3,2,1,0:T(8,128)S(1)} custom-call(f32[16,32,32,128]{3,2,1,0:T(8,128)} %spectrum.1.sums_ref, f32[8,1024,128]{2,1,0:T(8,128)S(1)} %get-tuple-element.21.first_ref, f32[8,1024,128]{2,1,0:T(8,128)} %get-tuple-element.22.last_ref), custom_call_target="tpu_custom_call" | custom-call | tf_op jit(solution)/shard_map/ends/pallas_call | solution.py:433
  36.6 0.3 reshape.65
  36.9 0.8 copy.11
  37.7 1.3 reshape.66
  39.0 0.6 gather_fusion
  39.6 0.1 copy_select_fusion
  39.7 3.8 %collective-permute-start.1 = (f32[8,2,8,128]{3,2,1,0:T(8,128)S(1)}, f32[8,2,8,128]{3,2,1,0:T(8,128)S(1)}, u32[]{:S(2)}, u32[]{:S(2)}) collective-permute-start(f32[8,2,8,128]{3,2,1,0:T(8,128)S(1)} %slice_bitcast_fusion), channel_id=1, source_target_pairs={{0,32},{16,48},{32,0},{48,16},{64,96},{80,112},{96,64},{112,80},{1... | collective-permute-start | bytes 196616 | tf_op jit(solution)/shard_map/ppermute | solution.py:453
  43.5 4.2 %collective-permute-done.1 = f32[8,2,8,128]{3,2,1,0:T(8,128)S(1)} collective-permute-done((f32[8,2,8,128]{3,2,1,0:T(8,128)S(1)}, f32[8,2,8,128]{3,2,1,0:T(8,128)S(1)}, u32[]{:S(2)}, u32[]{:S(2)}) %collective-permute-start.1) | collective-permute-done | bytes 65568 | tf_op jit(solution)/shard_map/ppermute | solution.py:453
  47.7 5.2 %collective-permute-start.2 = (f32[4,2,8,128]{3,2,1,0:T(8,128)S(1)}, f32[4,2,8,128]{3,2,1,0:T(8,128)S(1)}, u32[]{:S(2)}, u32[]{:S(2)}) collective-permute-start(f32[4,2,8,128]{3,2,1,0:T(8,128)S(1)} %slice_bitcast_fusion.2), channel_id=1, source_target_pairs={{0,64},{16,80},{32,96},{48,112},{64,0},{80,16},{96,32},{112,48},{1... | collective-permute-start | bytes 98312 | tf_op jit(solution)/shard_map/ppermute | solution.py:453
  52.9 2.8 %collective-permute-done.2 = f32[4,2,8,128]{3,2,1,0:T(8,128)S(1)} collective-permute-done((f32[4,2,8,128]{3,2,1,0:T(8,128)S(1)}, f32[4,2,8,128]{3,2,1,0:T(8,128)S(1)}, u32[]{:S(2)}, u32[]{:S(2)}) %collective-permute-start.2) | collective-permute-done | bytes 32800 | tf_op jit(solution)/shard_map/ppermute | solution.py:453
  55.7 8.8 %collective-permute-start.3 = (f32[2,2,8,128]{3,2,1,0:T(8,128)S(1)}, f32[2,2,8,128]{3,2,1,0:T(8,128)S(1)}, u32[]{:S(2)}, u32[]{:S(2)}) collective-permute-start(f32[2,2,8,128]{3,2,1,0:T(8,128)S(1)} %slice_bitcast_fusion.4), channel_id=1, source_target_pairs={{0,128},{16,144},{32,160},{48,176},{64,192},{80,208},{96,224},{112... | collective-permute-start | bytes 49160 | tf_op jit(solution)/shard_map/ppermute | solution.py:453
  64.5 2.3 %collective-permute-done.3 = f32[2,2,8,128]{3,2,1,0:T(8,128)S(1)} collective-permute-done((f32[2,2,8,128]{3,2,1,0:T(8,128)S(1)}, f32[2,2,8,128]{3,2,1,0:T(8,128)S(1)}, u32[]{:S(2)}, u32[]{:S(2)}) %collective-permute-start.3) | collective-permute-done | bytes 16416 | tf_op jit(solution)/shard_map/ppermute | solution.py:453
  66.8 14.8 %collective-permute-start.4 = (f32[1,2,8,128]{3,2,1,0:T(8,128)S(1)}, f32[1,2,8,128]{3,2,1,0:T(8,128)S(1)}, u32[]{:S(2)}, u32[]{:S(2)}) collective-permute-start(f32[1,2,8,128]{3,2,1,0:T(8,128)S(1)} %slice_bitcast_fusion.6), channel_id=1, source_target_pairs={{0,256},{16,272},{32,288},{48,304},{64,320},{80,336},{96,352},{112... | collective-permute-start | bytes 24584 | tf_op jit(solution)/shard_map/ppermute | solution.py:453
  81.6 2.0 %collective-permute-done.4 = f32[1,2,8,128]{3,2,1,0:T(8,128)S(1)} collective-permute-done((f32[1,2,8,128]{3,2,1,0:T(8,128)S(1)}, f32[1,2,8,128]{3,2,1,0:T(8,128)S(1)}, u32[]{:S(2)}, u32[]{:S(2)}) %collective-permute-start.4) | collective-permute-done | bytes 8224 | tf_op jit(solution)/shard_map/ppermute | solution.py:453
  83.6 0.7 broadcast_in_dim.20
  84.3 7.6 %all-to-all-start = ((f32[16,2,8,128]{3,2,1,0:T(8,128)}), f32[16,2,8,128]{3,2,1,0:T(8,128)S(1)}, u32[]{:S(2)}, u32[]{:S(2)}) async-start(f32[16,2,8,128]{3,2,1,0:T(8,128)} %broadcast_in_dim.20), calls=%async_computation.1 | async-start | bytes 262144 | tf_op jit(solution)/shard_map/all_to_all | solution.py:457
  91.9 0.1 dynamic_slice.7
  92.0 0.1 broadcast_in_dim_tile.3.modes_ref
  92.0 8.6 %carry.1.carry_ref = f32[6,16,8,128]{3,2,1,0:T(8,128)S(1)} custom-call(f32[2048]{0:T(1024)S(1)} %get-tuple-element.31.low_ref, f32[2048]{0:T(1024)S(1)} %get-tuple-element.32.up_ref, s32[1,128]{1,0:T(1,128)S(1)} %broadcast_in_dim_tile.3.modes_ref), custom_call_target="tpu_custom_call" | custom-call | tf_op jit(solution)/shard_map/carry/pallas_call | solution.py:461
  100.7 1.7 %own_factors.1 = (f32[128,8,128]{2,1,0:T(8,128)S(1)}, f32[128,8,128]{2,1,0:T(8,128)S(1)}, f32[128,8,128]{2,1,0:T(8,128)S(1)}) custom-call(s32[3]{0:T(128)S(1)} %pad_add_fusion.info_ref, f32[2048]{0:T(1024)S(1)} %get-tuple-element.31.low_ref, f32[2048]{0:T(1024)S(1)} %get-tuple-element.32.up_ref, s32[1,128]{1,0:T(1,128)S(1)} %broadcast_in_dim_tile.3.modes_ref), custom_call_target="tpu_custom_call" | custom-call | tf_op jit(solution)/shard_map/own_factors/pallas_call | solution.py:484
  102.3 0.0 all-to-all-done.ends_ref
  102.3 0.6 interfaces.1.edge_ref
  103.0 26.9 %reduce-scatter.2.cloned.1.call-done.sums_ref = f32[1024,128]{1,0:T(8,128)} async-done(((f32[16384,128]{1,0:T(8,128)}), f32[1024,128]{1,0:T(8,128)}) %reduce-scatter.2.cloned.1.call-update) | async-done | bytes 524304 | tf_op jit(solution)/shard_map/reduce_scatter | solution.py:412
  129.8 2.6 %solve.1 = f32[2,32,16,128]{3,2,1,0:T(8,128)} custom-call(s32[3]{0:T(128)S(1)} %pad_add_fusion.info_ref, f32[2048]{0:T(1024)S(1)} %get-tuple-element.31.low_ref, f32[2048]{0:T(1024)S(1)} %get-tuple-element.32.up_ref, f32[1024,128]{1,0:T(8,128)} %reduce-scatter.2.cloned.1.call-done.sums_ref, f32[2,8,128]{2,1,0:T(8,128)S(1)} %interfaces.1.edge_ref, ...), custom_call_target="tpu_custom_call" | custom-call | tf_op jit(solution)/shard_map/solve/pallas_call | solution.py:494
  (15 shorter events, 0.1 us)
Async XLA Ops:
  6.5 123.3 %reduce-scatter.2.cloned.1.call-start = ((), (), s32[]{:S(2)}) async-start(), calls=%async_computation.2 | async-start | bytes 8912896 | tf_op jit(solution)/shard_map/reduce_scatter | solution.py:412
  6.5 6.3 %collective-permute-start = (f32[32,128,128]{2,1,0:T(8,128)}, f32[32,128,128]{2,1,0:T(8,128)S(1)}, u32[]{:S(2)}, u32[]{:S(2)}) collective-permute-start(f32[32,128,128]{2,1,0:T(8,128)} %own_ref.1), channel_id=1, source_target_pairs={{0,16},{16,0},{32,48},{48,32},{64,80},{80,64},{96,112},{112,96},{1... | collective-permute-start | bytes 6291464 | tf_op jit(solution)/shard_map/ppermute | solution.py:375
  17.7 0.7 copy-start
  17.7 0.9 copy-start.1
  39.7 8.0 %collective-permute-start.1 = (f32[8,2,8,128]{3,2,1,0:T(8,128)S(1)}, f32[8,2,8,128]{3,2,1,0:T(8,128)S(1)}, u32[]{:S(2)}, u32[]{:S(2)}) collective-permute-start(f32[8,2,8,128]{3,2,1,0:T(8,128)S(1)} %slice_bitcast_fusion), channel_id=1, source_target_pairs={{0,32},{16,48},{32,0},{48,16},{64,96},{80,112},{96,64},{112,80},{1... | collective-permute-start | bytes 196616 | tf_op jit(solution)/shard_map/ppermute | solution.py:453
  47.7 8.0 %collective-permute-start.2 = (f32[4,2,8,128]{3,2,1,0:T(8,128)S(1)}, f32[4,2,8,128]{3,2,1,0:T(8,128)S(1)}, u32[]{:S(2)}, u32[]{:S(2)}) collective-permute-start(f32[4,2,8,128]{3,2,1,0:T(8,128)S(1)} %slice_bitcast_fusion.2), channel_id=1, source_target_pairs={{0,64},{16,80},{32,96},{48,112},{64,0},{80,16},{96,32},{112,48},{1... | collective-permute-start | bytes 98312 | tf_op jit(solution)/shard_map/ppermute | solution.py:453
  55.7 11.1 %collective-permute-start.3 = (f32[2,2,8,128]{3,2,1,0:T(8,128)S(1)}, f32[2,2,8,128]{3,2,1,0:T(8,128)S(1)}, u32[]{:S(2)}, u32[]{:S(2)}) collective-permute-start(f32[2,2,8,128]{3,2,1,0:T(8,128)S(1)} %slice_bitcast_fusion.4), channel_id=1, source_target_pairs={{0,128},{16,144},{32,160},{48,176},{64,192},{80,208},{96,224},{112... | collective-permute-start | bytes 49160 | tf_op jit(solution)/shard_map/ppermute | solution.py:453
  66.8 16.8 %collective-permute-start.4 = (f32[1,2,8,128]{3,2,1,0:T(8,128)S(1)}, f32[1,2,8,128]{3,2,1,0:T(8,128)S(1)}, u32[]{:S(2)}, u32[]{:S(2)}) collective-permute-start(f32[1,2,8,128]{3,2,1,0:T(8,128)S(1)} %slice_bitcast_fusion.6), channel_id=1, source_target_pairs={{0,256},{16,272},{32,288},{48,304},{64,320},{80,336},{96,352},{112... | collective-permute-start | bytes 24584 | tf_op jit(solution)/shard_map/ppermute | solution.py:453
  84.3 18.0 %all-to-all-start = ((f32[16,2,8,128]{3,2,1,0:T(8,128)}), f32[16,2,8,128]{3,2,1,0:T(8,128)S(1)}, u32[]{:S(2)}, u32[]{:S(2)}) async-start(f32[16,2,8,128]{3,2,1,0:T(8,128)} %broadcast_in_dim.20), calls=%async_computation.1 | async-start | bytes 262144 | tf_op jit(solution)/shard_map/all_to_all | solution.py:457
Sparse Core Ops, SparseCore 0:
  17.9 111.9 reduce-scatter.1

commit v4 on v3

--- a/solution.py
+++ b/solution.py
@@ -53,7 +53,7 @@
 
 
 def table_kernel(
-    length, info_ref, modes_ref, own_ref, high_ref, low_ref, own_high_ref, own_low_ref, own, sems
+    length, info_ref, modes_ref, own_ref, table_ref, own_high_ref, own_low_ref, own, sems
 ):
     core, index = info_ref[0], info_ref[2]
     steps = sems.shape[0]
@@ -65,31 +65,32 @@
     ]
     for load in loads:
         load.start()
-    chips = high_ref.shape[0]
+    chips = table_ref.shape[0]
     mode_column = jnp.concatenate([modes_ref[2 * chip + core] for chip in range(chips)], 0)
     for side in range(2):
         start = 128 * (index ^ side)
         place = start + lax.broadcasted_iota(jnp.int32, (1, 128), 1)
         real, imag = wave(mode_column * place, length)
         scale = 1.0 / math.sqrt(length)
-        columns = pl.ds(side * 128, 128)
         for part, values in enumerate((real * scale, imag * -scale)):
             high, low = halves(values)
-            high_ref[:, part, :, columns] = high.reshape(-1, 16, 128)
-            low_ref[:, part, :, columns] = low.reshape(-1, 16, 128)
+            for third, half in enumerate((high, high, low)):
+                columns = pl.ds(third * 256 + side * 128, 128)
+                table_ref[:, part, :, columns] = half.reshape(-1, 16, 128)
     for g in range(steps):
         loads[g].wait()
         own_high_ref[groups[g]], own_low_ref[groups[g]] = halves(own[groups[g]])
 
 
-def spectrum_kernel(
-    high_ref, low_ref, own_high_ref, own_low_ref, got_ref, out_ref, sums, out_sems
-):
-    slots, chips, some = sums.shape[:3]
-    steps = got_ref.shape[0] // some
+def spectrum_kernel(plan, table_ref, own_high_ref, own_low_ref, got_ref, out_ref, sums, out_sems):
+    slots, chips = sums.shape[:2]
+    steps = len(plan)
+    bounds = [sum(plan[:g]) for g in range(steps)]
     stores = [
         pltpu.make_async_copy(
-            sums.at[g % slots], out_ref.at[:, pl.ds(some * g, some)], out_sems.at[g % slots]
+            sums.at[g % slots, :, pl.ds(0, plan[g])],
+            out_ref.at[:, pl.ds(bounds[g], plan[g])],
+            out_sems.at[g % slots],
         )
         for g in range(steps)
     ]
@@ -100,18 +101,16 @@
     for g in range(steps):
         if g >= slots:
             stores[g - slots].wait()
-        for pair in range(0, some, 2):
-            plane = some * g + pair
+        for pair in range(0, plan[g], 2):
+            plane = bounds[g] + pair
             got_high, got_low = halves(beside(got_ref, plane))
             field_high = jnp.concatenate([beside(own_high_ref, plane), got_high], 0)
             field_low = jnp.concatenate([beside(own_low_ref, plane), got_low], 0)
+            fields = jnp.concatenate([field_high, field_low, field_high], 0)
             step = 8
             for first in range(0, chips, step):
                 rows = pl.ds(first * 32, step * 32)
-                high = high_ref[rows, :]
-                total = jnp.dot(high, field_high, preferred_element_type=F32)
-                total += jnp.dot(high, field_low, preferred_element_type=F32)
-                total += jnp.dot(low_ref[rows, :], field_high, preferred_element_type=F32)
+                total = jnp.dot(table_ref[rows, :], fields, preferred_element_type=F32)
                 for k in range(2):
                     piece = total[:, k * 128 : (k + 1) * 128].reshape(step, 32, 128)
                     sums[g % slots, pl.ds(first, step), pair + k] = piece
@@ -375,34 +374,33 @@
     got = lax.ppermute(source, "gx", [(i, i ^ 1) for i in range(gx_count)])
     hbm = pl.BlockSpec(memory_space=pltpu.HBM)
     source = pltpu.with_memory_space_constraint(source, pltpu.HBM)
-    table_shape = jax.ShapeDtypeStruct((chips, 2, 16, 256), BF16)
+    table_shape = jax.ShapeDtypeStruct((chips, 2, 16, 768), BF16)
     own_shape = jax.ShapeDtypeStruct(source.shape, BF16)
-    table_high, table_low, own_high, own_low = pl.pallas_call(
+    table, own_high, own_low = pl.pallas_call(
         functools.partial(table_kernel, length),
-        out_shape=(table_shape, table_shape, own_shape, own_shape),
+        out_shape=(table_shape, own_shape, own_shape),
         in_specs=[SMEM, VMEM, hbm],
-        out_specs=(VMEM,) * 4,
+        out_specs=(VMEM,) * 3,
         scratch_shapes=[pltpu.VMEM(source.shape, F32), pltpu.SemaphoreType.DMA((4,))],
         compiler_params=PARAMS,
         name="tables",
     )(info, mode_index.reshape(gx_count, 16, 1), source)
 
-    some = 8
+    plan = (4, 8, 8, 8, 4)
     slots = 3
     partial_sums = pl.pallas_call(
-        spectrum_kernel,
+        functools.partial(spectrum_kernel, plan),
         out_shape=jax.ShapeDtypeStruct((chips, planes, 32, wall_rows), F32),
-        in_specs=[VMEM] * 5,
+        in_specs=[VMEM] * 4,
         out_specs=hbm,
         scratch_shapes=[
-            pltpu.VMEM((slots, chips, some, 32, wall_rows), F32),
+            pltpu.VMEM((slots, chips, max(plan), 32, wall_rows), F32),
             pltpu.SemaphoreType.DMA((slots,)),
         ],
         compiler_params=PARAMS,
         name="spectrum",
     )(
-        table_high.reshape(chips * 32, 256),
-        table_low.reshape(chips * 32, 256),
+        table.reshape(chips * 32, 768),
         own_high,
         own_low,
         got,

time: 140 us -> 140 us (level)
  no operation moved by 1% of the time
where the time goes in v4:
time: 140 us; the launch traced here: 139 us
  starting transfers between devices  42.1 us (30%)
  waiting for transfers between devices  39.3 us (28%)
  Pallas kernels  38.2 us (27%)
  between operations  13.6 us (10%)
  local copies, waits for them, and re-layouts  5.57 us (4%)
    ppermute x4, starting transfers between devices, local(): ends = pairs[:, 0] + lax.ppermute(pairs[:, 1], 'gx', route)  32.6 us
    reduce_scatter x1, waiting for transfers between devices, local(): lax.psum_scatter(partial_sums.reshape(chips * planes * 32, wall_rows), 'g...  26.9 us
    ppermute x4, waiting for transfers between devices, local(): ends = pairs[:, 0] + lax.ppermute(pairs[:, 1], 'gx', route)  11.2 us
    pallas_call x1, Pallas kernels, local(): pl.pallas_call(weights_kernel, out_shape=(weights, weights), in_specs=[SM...  9.69 us
    pallas_call x1, Pallas kernels, local(): pl.pallas_call(carry_kernel, out_shape=jax.ShapeDtypeStruct((6, gy_count,...  8.61 us
    pallas_call x1, Pallas kernels, local(): pl.pallas_call(ends_kernel, out_shape=jax.ShapeDtypeStruct((2, 2, groups...  8.05 us
    all_to_all x1, starting transfers between devices, local(): lax.all_to_all(copies, 'gy', split_axis=0, concat_axis=0, tiled=True)  7.61 us
    pallas_call x1, Pallas kernels, local(): pl.pallas_call(functools.partial(spectrum_kernel, plan), out_shape=jax.Sh...  4.82 us
  transfers between devices with their start and end apart: 7, of which 6 were waited for; matrix products, arithmetic and copies ran while one was open for 4% of the time, Pallas kernels for 22%

profile of v4, /device:TPU:24, one launch (start us, length us, event | category | flops | bytes accessed | tf_op | source)
XLA Modules:
  0.0 139.1 jit_solution(923086843879952860)
XLA Ops:
  6.5 0.0 reduce-scatter.2.cloned.1.call-start
  6.5 1.9 %collective-permute-start = (f32[32,128,128]{2,1,0:T(8,128)}, f32[32,128,128]{2,1,0:T(8,128)S(1)}, u32[]{:S(2)}, u32[]{:S(2)}) collective-permute-start(f32[32,128,128]{2,1,0:T(8,128)} %own_ref.1), channel_id=1, source_target_pairs={{0,16},{16,0},{32,48},{48,32},{64,80},{80,64},{96,112},{112,96},{1... | collective-permute-start | bytes 6291464 | tf_op jit(solution)/shard_map/ppermute | solution.py:374
  8.5 0.9 reshape.74.modes_ref
  9.4 0.1 pad_add_fusion.info_ref
  9.4 2.2 %tables.1 = (bf16[16,2,16,768]{3,2,1,0:T(8,128)(2,1)S(1)}, bf16[32,128,128]{2,1,0:T(8,128)(2,1)S(1)}, bf16[32,128,128]{2,1,0:T(8,128)(2,1)S(1)}) custom-call(s32[3]{0:T(128)S(1)} %pad_add_fusion.info_ref, s32[32,16,1]{2,1,0:T(8,128)S(1)} %reshape.74.modes_ref, f32[32,128,128]{2,1,0:T(8,128)} %own_ref.1), custom_call_target="tpu_custom_call" | custom-call | tf_op jit(solution)/shard_map/tables/pallas_call | solution.py:379
  11.6 1.2 collective-permute-done.got_ref
  12.8 4.8 %spectrum.1.sums_ref = f32[16,32,32,128]{3,2,1,0:T(8,128)} custom-call(bf16[512,768]{1,0:T(8,128)(2,1)S(1)} %bitcast.50, bf16[32,128,128]{2,1,0:T(8,128)(2,1)S(1)} %get-tuple-element.17.own_high_ref, bf16[32,128,128]{2,1,0:T(8,128)(2,1)S(1)} %get-tuple-element.18.own_low_ref, f32[32,128,128]{2,1,0:T(8,128)S(1)} %collective-permute-done.got_ref), custom_call_target="tpu_custom_call" | custom-call | tf_op jit(solution)/shard_map/spectrum/pallas_call | solution.py:391
  17.6 0.0 copy-start
  17.6 0.0 copy-start.1
  17.6 0.0 reduce-scatter.2.cloned.1.call-update
  17.7 0.6 copy-done
  18.3 0.1 reshape.60
  18.4 0.1 tile.16
  18.5 0.0 copy-done.1
  18.5 0.1 multiply_divide_fusion
  18.6 0.1 pad_maximum_fusion
  18.7 9.7 %weights.1 = (f32[8,1024,128]{2,1,0:T(8,128)S(1)}, f32[8,1024,128]{2,1,0:T(8,128)}) custom-call(s32[3]{0:T(128)S(1)} %pad_add_fusion.info_ref, f32[2048]{0:T(1024)S(1)} %get-tuple-element.29.low_ref, f32[2048]{0:T(1024)S(1)} %get-tuple-element.30.up_ref, s32[8,128]{1,0:T(8,128)S(1)} %bitcast.51), custom_call_target="tpu_custom_call" | custom-call | tf_op jit(solution)/shard_map/weights/pallas_call | solution.py:422
  28.4 8.0 %ends.1 = f32[2,2,64,128]{3,2,1,0:T(8,128)S(1)} custom-call(f32[16,32,32,128]{3,2,1,0:T(8,128)} %spectrum.1.sums_ref, f32[8,1024,128]{2,1,0:T(8,128)S(1)} %get-tuple-element.19.first_ref, f32[8,1024,128]{2,1,0:T(8,128)} %get-tuple-element.20.last_ref), custom_call_target="tpu_custom_call" | custom-call | tf_op jit(solution)/shard_map/ends/pallas_call | solution.py:431
  36.5 0.3 reshape.61
  36.8 0.8 copy.11
  37.6 1.3 reshape.62
  38.9 0.6 gather_fusion
  39.5 0.1 copy_select_fusion
  39.6 3.8 %collective-permute-start.1 = (f32[8,2,8,128]{3,2,1,0:T(8,128)S(1)}, f32[8,2,8,128]{3,2,1,0:T(8,128)S(1)}, u32[]{:S(2)}, u32[]{:S(2)}) collective-permute-start(f32[8,2,8,128]{3,2,1,0:T(8,128)S(1)} %slice_bitcast_fusion), channel_id=1, source_target_pairs={{0,32},{16,48},{32,0},{48,16},{64,96},{80,112},{96,64},{112,80},{1... | collective-permute-start | bytes 196616 | tf_op jit(solution)/shard_map/ppermute | solution.py:451
  43.4 4.2 %collective-permute-done.1 = f32[8,2,8,128]{3,2,1,0:T(8,128)S(1)} collective-permute-done((f32[8,2,8,128]{3,2,1,0:T(8,128)S(1)}, f32[8,2,8,128]{3,2,1,0:T(8,128)S(1)}, u32[]{:S(2)}, u32[]{:S(2)}) %collective-permute-start.1) | collective-permute-done | bytes 65568 | tf_op jit(solution)/shard_map/ppermute | solution.py:451
  47.6 5.2 %collective-permute-start.2 = (f32[4,2,8,128]{3,2,1,0:T(8,128)S(1)}, f32[4,2,8,128]{3,2,1,0:T(8,128)S(1)}, u32[]{:S(2)}, u32[]{:S(2)}) collective-permute-start(f32[4,2,8,128]{3,2,1,0:T(8,128)S(1)} %slice_bitcast_fusion.2), channel_id=1, source_target_pairs={{0,64},{16,80},{32,96},{48,112},{64,0},{80,16},{96,32},{112,48},{1... | collective-permute-start | bytes 98312 | tf_op jit(solution)/shard_map/ppermute | solution.py:451
  52.8 2.8 %collective-permute-done.2 = f32[4,2,8,128]{3,2,1,0:T(8,128)S(1)} collective-permute-done((f32[4,2,8,128]{3,2,1,0:T(8,128)S(1)}, f32[4,2,8,128]{3,2,1,0:T(8,128)S(1)}, u32[]{:S(2)}, u32[]{:S(2)}) %collective-permute-start.2) | collective-permute-done | bytes 32800 | tf_op jit(solution)/shard_map/ppermute | solution.py:451
  55.6 8.8 %collective-permute-start.3 = (f32[2,2,8,128]{3,2,1,0:T(8,128)S(1)}, f32[2,2,8,128]{3,2,1,0:T(8,128)S(1)}, u32[]{:S(2)}, u32[]{:S(2)}) collective-permute-start(f32[2,2,8,128]{3,2,1,0:T(8,128)S(1)} %slice_bitcast_fusion.4), channel_id=1, source_target_pairs={{0,128},{16,144},{32,160},{48,176},{64,192},{80,208},{96,224},{112... | collective-permute-start | bytes 49160 | tf_op jit(solution)/shard_map/ppermute | solution.py:451
  64.4 2.3 %collective-permute-done.3 = f32[2,2,8,128]{3,2,1,0:T(8,128)S(1)} collective-permute-done((f32[2,2,8,128]{3,2,1,0:T(8,128)S(1)}, f32[2,2,8,128]{3,2,1,0:T(8,128)S(1)}, u32[]{:S(2)}, u32[]{:S(2)}) %collective-permute-start.3) | collective-permute-done | bytes 16416 | tf_op jit(solution)/shard_map/ppermute | solution.py:451
  66.7 14.8 %collective-permute-start.4 = (f32[1,2,8,128]{3,2,1,0:T(8,128)S(1)}, f32[1,2,8,128]{3,2,1,0:T(8,128)S(1)}, u32[]{:S(2)}, u32[]{:S(2)}) collective-permute-start(f32[1,2,8,128]{3,2,1,0:T(8,128)S(1)} %slice_bitcast_fusion.6), channel_id=1, source_target_pairs={{0,256},{16,272},{32,288},{48,304},{64,320},{80,336},{96,352},{112... | collective-permute-start | bytes 24584 | tf_op jit(solution)/shard_map/ppermute | solution.py:451
  81.5 2.0 %collective-permute-done.4 = f32[1,2,8,128]{3,2,1,0:T(8,128)S(1)} collective-permute-done((f32[1,2,8,128]{3,2,1,0:T(8,128)S(1)}, f32[1,2,8,128]{3,2,1,0:T(8,128)S(1)}, u32[]{:S(2)}, u32[]{:S(2)}) %collective-permute-start.4) | collective-permute-done | bytes 8224 | tf_op jit(solution)/shard_map/ppermute | solution.py:451
  83.5 0.7 broadcast_in_dim.20
  84.2 7.6 %all-to-all-start = ((f32[16,2,8,128]{3,2,1,0:T(8,128)}), f32[16,2,8,128]{3,2,1,0:T(8,128)S(1)}, u32[]{:S(2)}, u32[]{:S(2)}) async-start(f32[16,2,8,128]{3,2,1,0:T(8,128)} %broadcast_in_dim.20), calls=%async_computation.1 | async-start | bytes 262144 | tf_op jit(solution)/shard_map/all_to_all | solution.py:455
  91.8 0.1 dynamic_slice.7
  91.9 0.1 broadcast_in_dim_tile.3.modes_ref
  92.0 8.6 %carry.1.carry_ref = f32[6,16,8,128]{3,2,1,0:T(8,128)S(1)} custom-call(f32[2048]{0:T(1024)S(1)} %get-tuple-element.29.low_ref, f32[2048]{0:T(1024)S(1)} %get-tuple-element.30.up_ref, s32[1,128]{1,0:T(1,128)S(1)} %broadcast_in_dim_tile.3.modes_ref), custom_call_target="tpu_custom_call" | custom-call | tf_op jit(solution)/shard_map/carry/pallas_call | solution.py:459
  100.6 1.7 %own_factors.1 = (f32[128,8,128]{2,1,0:T(8,128)S(1)}, f32[128,8,128]{2,1,0:T(8,128)S(1)}, f32[128,8,128]{2,1,0:T(8,128)S(1)}) custom-call(s32[3]{0:T(128)S(1)} %pad_add_fusion.info_ref, f32[2048]{0:T(1024)S(1)} %get-tuple-element.29.low_ref, f32[2048]{0:T(1024)S(1)} %get-tuple-element.30.up_ref, s32[1,128]{1,0:T(1,128)S(1)} %broadcast_in_dim_tile.3.modes_ref), custom_call_target="tpu_custom_call" | custom-call | tf_op jit(solution)/shard_map/own_factors/pallas_call | solution.py:482
  102.3 0.0 all-to-all-done.ends_ref
  102.3 0.6 interfaces.1.edge_ref
  102.9 26.9 %reduce-scatter.2.cloned.1.call-done.sums_ref = f32[1024,128]{1,0:T(8,128)} async-done(((f32[16384,128]{1,0:T(8,128)}), f32[1024,128]{1,0:T(8,128)}) %reduce-scatter.2.cloned.1.call-update) | async-done | bytes 524304 | tf_op jit(solution)/shard_map/reduce_scatter | solution.py:410
  129.7 2.6 %solve.1 = f32[2,32,16,128]{3,2,1,0:T(8,128)} custom-call(s32[3]{0:T(128)S(1)} %pad_add_fusion.info_ref, f32[2048]{0:T(1024)S(1)} %get-tuple-element.29.low_ref, f32[2048]{0:T(1024)S(1)} %get-tuple-element.30.up_ref, f32[1024,128]{1,0:T(8,128)} %reduce-scatter.2.cloned.1.call-done.sums_ref, f32[2,8,128]{2,1,0:T(8,128)S(1)} %interfaces.1.edge_ref, ...), custom_call_target="tpu_custom_call" | custom-call | tf_op jit(solution)/shard_map/solve/pallas_call | solution.py:492
  (15 shorter events, 0.1 us)
Async XLA Ops:
  6.5 123.2 %reduce-scatter.2.cloned.1.call-start = ((), (), s32[]{:S(2)}) async-start(), calls=%async_computation.2 | async-start | bytes 8912896 | tf_op jit(solution)/shard_map/reduce_scatter | solution.py:410
  6.5 6.3 %collective-permute-start = (f32[32,128,128]{2,1,0:T(8,128)}, f32[32,128,128]{2,1,0:T(8,128)S(1)}, u32[]{:S(2)}, u32[]{:S(2)}) collective-permute-start(f32[32,128,128]{2,1,0:T(8,128)} %own_ref.1), channel_id=1, source_target_pairs={{0,16},{16,0},{32,48},{48,32},{64,80},{80,64},{96,112},{112,96},{1... | collective-permute-start | bytes 6291464 | tf_op jit(solution)/shard_map/ppermute | solution.py:374
  17.6 0.7 copy-start
  17.6 0.9 copy-start.1
  39.6 8.0 %collective-permute-start.1 = (f32[8,2,8,128]{3,2,1,0:T(8,128)S(1)}, f32[8,2,8,128]{3,2,1,0:T(8,128)S(1)}, u32[]{:S(2)}, u32[]{:S(2)}) collective-permute-start(f32[8,2,8,128]{3,2,1,0:T(8,128)S(1)} %slice_bitcast_fusion), channel_id=1, source_target_pairs={{0,32},{16,48},{32,0},{48,16},{64,96},{80,112},{96,64},{112,80},{1... | collective-permute-start | bytes 196616 | tf_op jit(solution)/shard_map/ppermute | solution.py:451
  47.6 8.0 %collective-permute-start.2 = (f32[4,2,8,128]{3,2,1,0:T(8,128)S(1)}, f32[4,2,8,128]{3,2,1,0:T(8,128)S(1)}, u32[]{:S(2)}, u32[]{:S(2)}) collective-permute-start(f32[4,2,8,128]{3,2,1,0:T(8,128)S(1)} %slice_bitcast_fusion.2), channel_id=1, source_target_pairs={{0,64},{16,80},{32,96},{48,112},{64,0},{80,16},{96,32},{112,48},{1... | collective-permute-start | bytes 98312 | tf_op jit(solution)/shard_map/ppermute | solution.py:451
  55.6 11.1 %collective-permute-start.3 = (f32[2,2,8,128]{3,2,1,0:T(8,128)S(1)}, f32[2,2,8,128]{3,2,1,0:T(8,128)S(1)}, u32[]{:S(2)}, u32[]{:S(2)}) collective-permute-start(f32[2,2,8,128]{3,2,1,0:T(8,128)S(1)} %slice_bitcast_fusion.4), channel_id=1, source_target_pairs={{0,128},{16,144},{32,160},{48,176},{64,192},{80,208},{96,224},{112... | collective-permute-start | bytes 49160 | tf_op jit(solution)/shard_map/ppermute | solution.py:451
  66.7 16.8 %collective-permute-start.4 = (f32[1,2,8,128]{3,2,1,0:T(8,128)S(1)}, f32[1,2,8,128]{3,2,1,0:T(8,128)S(1)}, u32[]{:S(2)}, u32[]{:S(2)}) collective-permute-start(f32[1,2,8,128]{3,2,1,0:T(8,128)S(1)} %slice_bitcast_fusion.6), channel_id=1, source_target_pairs={{0,256},{16,272},{32,288},{48,304},{64,320},{80,336},{96,352},{112... | collective-permute-start | bytes 24584 | tf_op jit(solution)/shard_map/ppermute | solution.py:451
  84.2 18.1 %all-to-all-start = ((f32[16,2,8,128]{3,2,1,0:T(8,128)}), f32[16,2,8,128]{3,2,1,0:T(8,128)S(1)}, u32[]{:S(2)}, u32[]{:S(2)}) async-start(f32[16,2,8,128]{3,2,1,0:T(8,128)} %broadcast_in_dim.20), calls=%async_computation.1 | async-start | bytes 262144 | tf_op jit(solution)/shard_map/all_to_all | solution.py:455
Sparse Core Ops, SparseCore 0:
  17.8 111.9 reduce-scatter.1

commit v5 on v3

--- a/solution.py
+++ b/solution.py
@@ -239,7 +239,7 @@
             ends_ref[1, part, pl.ds(row, 1), :] = jnp.sum(values * last, 0, keepdims=True)
 
 
-def interface_kernel(info_ref, ends_ref, carry_ref, edge_ref, sums, firsts):
+def interface_kernel(info_ref, low_ref, up_ref, ends_ref, carry_ref, edge_ref, sums, firsts):
     block = info_ref[1]
     blocks = ends_ref.shape[0]
     before = jnp.zeros((8, 128), F32)
@@ -252,8 +252,9 @@
         base = carry_ref[2, b] * ends_ref[b, 0] + carry_ref[3, b] * sums[b]
         after = base + carry_ref[4, b] * after
     firsts[0] = after
-    edge_ref[0] = sums[block] + carry_ref[5, block] * firsts[block]
-    edge_ref[1] = firsts[block + 1]
+    below = sums[block] + carry_ref[5, block] * firsts[block]
+    edge_ref[0] = low_ref[128 * block] * below
+    edge_ref[1] = up_ref[128 * block + 127] * firsts[block + 1]
 
 
 def own_factor_kernel(info_ref, low_ref, up_ref, modes_ref, ratio_ref, inverse_ref, back_ref):
@@ -299,9 +300,6 @@
 
 
 def solve_kernel(
-    info_ref,
-    low_ref,
-    up_ref,
     sums_ref,
     edge_ref,
     ratio_ref,
@@ -312,15 +310,14 @@
 ):
     rows = 128
     half = rows // 2
-    start = info_ref[1] * rows
     for k in range(8):
         work[pl.ds(k, rows, stride=8), :] = sums_ref[pl.ds(rows * k, rows), :].T
 
     def row(j):
         return pl.ds(pl.multiple_of(j * 8, 8), 8)
 
-    upper = work[row(0), :] + low_ref[start] * edge_ref[0]
-    lower = work[row(rows - 1), :] + up_ref[start + rows - 1] * edge_ref[1]
+    upper = work[row(0), :] + edge_ref[0]
+    lower = work[row(rows - 1), :] + edge_ref[1]
     work[row(0), :] = upper
     work[row(rows - 1), :] = lower
 
@@ -470,7 +467,7 @@
     edges = pl.pallas_call(
         interface_kernel,
         out_shape=jax.ShapeDtypeStruct((2, 8, 128), F32),
-        in_specs=[SMEM, VMEM, VMEM],
+        in_specs=[SMEM] * 3 + [VMEM] * 2,
         out_specs=VMEM,
         scratch_shapes=[
             pltpu.VMEM((gy_count, 8, 128), F32),
@@ -478,7 +475,7 @@
         ],
         compiler_params=PARAMS,
         name="interfaces",
-    )(info, all_ends, carry)
+    )(info, lower_all, upper_all, all_ends, carry)
 
     column = jax.ShapeDtypeStruct((wall_rows, 8, 128), F32)
     ratio, inverse, back = pl.pallas_call(
@@ -494,15 +491,12 @@
     return pl.pallas_call(
         solve_kernel,
         out_shape=jax.ShapeDtypeStruct((2, planes, 16, wall_rows), F32),
-        in_specs=[SMEM] * 3 + [VMEM] * 5,
+        in_specs=[VMEM] * 5,
         out_specs=VMEM,
         scratch_shapes=[pltpu.VMEM((planes * 32, wall_rows), F32)],
         compiler_params=PARAMS,
         name="solve",
     )(
-        info,
-        lower_all,
-        upper_all,
         pltpu.with_memory_space_constraint(summed, pltpu.HBM),
         edges,
         ratio,

time: 140 us -> 140 us (level)
  no operation moved by 1% of the time
where the time goes in v5:
time: 140 us; the launch traced here: 139 us
  starting transfers between devices  42.1 us (30%)
  waiting for transfers between devices  39 us (28%)
  Pallas kernels  38.5 us (28%)
  between operations  13.6 us (10%)
  local copies, waits for them, and re-layouts  5.57 us (4%)
    ppermute x4, starting transfers between devices, local(): ends = pairs[:, 0] + lax.ppermute(pairs[:, 1], 'gx', route)  32.6 us
    reduce_scatter x1, waiting for transfers between devices, local(): lax.psum_scatter(partial_sums.reshape(chips * planes * 32, wall_rows), 'g...  26.6 us
    ppermute x4, waiting for transfers between devices, local(): ends = pairs[:, 0] + lax.ppermute(pairs[:, 1], 'gx', route)  11.2 us
    pallas_call x1, Pallas kernels, local(): pl.pallas_call(weights_kernel, out_shape=(weights, weights), in_specs=[SM...  9.69 us
    pallas_call x1, Pallas kernels, local(): pl.pallas_call(carry_kernel, out_shape=jax.ShapeDtypeStruct((6, gy_count,...  8.61 us
    pallas_call x1, Pallas kernels, local(): pl.pallas_call(ends_kernel, out_shape=jax.ShapeDtypeStruct((2, 2, groups...  8.05 us
    all_to_all x1, starting transfers between devices, local(): lax.all_to_all(copies, 'gy', split_axis=0, concat_axis=0, tiled=True)  7.6 us
    pallas_call x1, Pallas kernels, local(): pl.pallas_call(spectrum_kernel, out_shape=jax.ShapeDtypeStruct((chips, pl...  4.91 us
  transfers between devices with their start and end apart: 7, of which 6 were waited for; matrix products, arithmetic and copies ran while one was open for 4% of the time, Pallas kernels for 22%

profile of v5, /device:TPU:24, one launch (start us, length us, event | category | flops | bytes accessed | tf_op | source)
XLA Modules:
  0.0 139.2 jit_solution(17406772827726682143)
XLA Ops:
  6.5 0.0 reduce-scatter.2.cloned.1.call-start
  6.5 1.9 %collective-permute-start = (f32[32,128,128]{2,1,0:T(8,128)}, f32[32,128,128]{2,1,0:T(8,128)S(1)}, u32[]{:S(2)}, u32[]{:S(2)}) collective-permute-start(f32[32,128,128]{2,1,0:T(8,128)} %own_ref.1), channel_id=1, source_target_pairs={{0,16},{16,0},{32,48},{48,32},{64,80},{80,64},{96,112},{112,96},{1... | collective-permute-start | bytes 6291464 | tf_op jit(solution)/shard_map/ppermute | solution.py:372
  8.5 0.9 reshape.78.modes_ref
  9.4 0.1 pad_add_fusion.info_ref
  9.4 2.2 %tables.1 = (bf16[16,2,16,256]{3,2,1,0:T(8,128)(2,1)S(1)}, bf16[16,2,16,256]{3,2,1,0:T(8,128)(2,1)S(1)}, bf16[32,128,128]{2,1,0:T(8,128)(2,1)S(1)}, bf16[32,128,128]{2,1,0:T(8,128)(2,1)S(1)}) custom-call(s32[3]{0:T(128)S(1)} %pad_add_fusion.info_ref, s32[32,16,1]{2,1,0:T(8,128)S(1)} %reshape.78.modes_ref, f32[32,128,128]{2,1,0:T(8,128)} %own_ref.1), custom_call_target="tpu_custom_call" | custom-call | tf_op jit(solution)/shard_map/tables/pallas_call | solution.py:377
  11.6 1.2 collective-permute-done.got_ref
  12.8 4.9 %spectrum.1.sums_ref = f32[16,32,32,128]{3,2,1,0:T(8,128)} custom-call(bf16[512,256]{1,0:T(8,128)(2,1)S(1)} %bitcast.51, bf16[512,256]{1,0:T(8,128)(2,1)S(1)} %bitcast.52, bf16[32,128,128]{2,1,0:T(8,128)(2,1)S(1)} %get-tuple-element.19.own_high_ref, bf16[32,128,128]{2,1,0:T(8,128)(2,1)S(1)} %get-tuple-element.20.own_low_ref, ...), custom_call_target="tpu_custom_call" | custom-call | tf_op jit(solution)/shard_map/spectrum/pallas_call | solution.py:389
  17.7 0.0 copy-start
  17.7 0.0 copy-start.1
  17.7 0.0 reduce-scatter.2.cloned.1.call-update
  17.8 0.6 copy-done
  18.4 0.1 reshape.64
  18.5 0.1 tile.16
  18.6 0.0 copy-done.1
  18.6 0.1 multiply_divide_fusion
  18.7 0.1 pad_maximum_fusion
  18.8 9.7 %weights.1 = (f32[8,1024,128]{2,1,0:T(8,128)S(1)}, f32[8,1024,128]{2,1,0:T(8,128)}) custom-call(s32[3]{0:T(128)S(1)} %pad_add_fusion.info_ref, f32[2048]{0:T(1024)S(1)} %get-tuple-element.31.low_ref, f32[2048]{0:T(1024)S(1)} %get-tuple-element.32.up_ref, s32[8,128]{1,0:T(8,128)S(1)} %bitcast.53), custom_call_target="tpu_custom_call" | custom-call | tf_op jit(solution)/shard_map/weights/pallas_call | solution.py:421
  28.5 8.0 %ends.1 = f32[2,2,64,128]{3,2,1,0:T(8,128)S(1)} custom-call(f32[16,32,32,128]{3,2,1,0:T(8,128)} %spectrum.1.sums_ref, f32[8,1024,128]{2,1,0:T(8,128)S(1)} %get-tuple-element.21.first_ref, f32[8,1024,128]{2,1,0:T(8,128)} %get-tuple-element.22.last_ref), custom_call_target="tpu_custom_call" | custom-call | tf_op jit(solution)/shard_map/ends/pallas_call | solution.py:430
  36.6 0.3 reshape.65
  36.9 0.8 copy.11
  37.7 1.3 reshape.66
  39.0 0.6 gather_fusion
  39.6 0.1 copy_select_fusion
  39.7 3.8 %collective-permute-start.1 = (f32[8,2,8,128]{3,2,1,0:T(8,128)S(1)}, f32[8,2,8,128]{3,2,1,0:T(8,128)S(1)}, u32[]{:S(2)}, u32[]{:S(2)}) collective-permute-start(f32[8,2,8,128]{3,2,1,0:T(8,128)S(1)} %slice_bitcast_fusion), channel_id=1, source_target_pairs={{0,32},{16,48},{32,0},{48,16},{64,96},{80,112},{96,64},{112,80},{1... | collective-permute-start | bytes 196616 | tf_op jit(solution)/shard_map/ppermute | solution.py:450
  43.5 4.2 %collective-permute-done.1 = f32[8,2,8,128]{3,2,1,0:T(8,128)S(1)} collective-permute-done((f32[8,2,8,128]{3,2,1,0:T(8,128)S(1)}, f32[8,2,8,128]{3,2,1,0:T(8,128)S(1)}, u32[]{:S(2)}, u32[]{:S(2)}) %collective-permute-start.1) | collective-permute-done | bytes 65568 | tf_op jit(solution)/shard_map/ppermute | solution.py:450
  47.7 5.2 %collective-permute-start.2 = (f32[4,2,8,128]{3,2,1,0:T(8,128)S(1)}, f32[4,2,8,128]{3,2,1,0:T(8,128)S(1)}, u32[]{:S(2)}, u32[]{:S(2)}) collective-permute-start(f32[4,2,8,128]{3,2,1,0:T(8,128)S(1)} %slice_bitcast_fusion.2), channel_id=1, source_target_pairs={{0,64},{16,80},{32,96},{48,112},{64,0},{80,16},{96,32},{112,48},{1... | collective-permute-start | bytes 98312 | tf_op jit(solution)/shard_map/ppermute | solution.py:450
  52.9 2.8 %collective-permute-done.2 = f32[4,2,8,128]{3,2,1,0:T(8,128)S(1)} collective-permute-done((f32[4,2,8,128]{3,2,1,0:T(8,128)S(1)}, f32[4,2,8,128]{3,2,1,0:T(8,128)S(1)}, u32[]{:S(2)}, u32[]{:S(2)}) %collective-permute-start.2) | collective-permute-done | bytes 32800 | tf_op jit(solution)/shard_map/ppermute | solution.py:450
  55.7 8.8 %collective-permute-start.3 = (f32[2,2,8,128]{3,2,1,0:T(8,128)S(1)}, f32[2,2,8,128]{3,2,1,0:T(8,128)S(1)}, u32[]{:S(2)}, u32[]{:S(2)}) collective-permute-start(f32[2,2,8,128]{3,2,1,0:T(8,128)S(1)} %slice_bitcast_fusion.4), channel_id=1, source_target_pairs={{0,128},{16,144},{32,160},{48,176},{64,192},{80,208},{96,224},{112... | collective-permute-start | bytes 49160 | tf_op jit(solution)/shard_map/ppermute | solution.py:450
  64.5 2.3 %collective-permute-done.3 = f32[2,2,8,128]{3,2,1,0:T(8,128)S(1)} collective-permute-done((f32[2,2,8,128]{3,2,1,0:T(8,128)S(1)}, f32[2,2,8,128]{3,2,1,0:T(8,128)S(1)}, u32[]{:S(2)}, u32[]{:S(2)}) %collective-permute-start.3) | collective-permute-done | bytes 16416 | tf_op jit(solution)/shard_map/ppermute | solution.py:450
  66.8 14.8 %collective-permute-start.4 = (f32[1,2,8,128]{3,2,1,0:T(8,128)S(1)}, f32[1,2,8,128]{3,2,1,0:T(8,128)S(1)}, u32[]{:S(2)}, u32[]{:S(2)}) collective-permute-start(f32[1,2,8,128]{3,2,1,0:T(8,128)S(1)} %slice_bitcast_fusion.6), channel_id=1, source_target_pairs={{0,256},{16,272},{32,288},{48,304},{64,320},{80,336},{96,352},{112... | collective-permute-start | bytes 24584 | tf_op jit(solution)/shard_map/ppermute | solution.py:450
  81.6 2.0 %collective-permute-done.4 = f32[1,2,8,128]{3,2,1,0:T(8,128)S(1)} collective-permute-done((f32[1,2,8,128]{3,2,1,0:T(8,128)S(1)}, f32[1,2,8,128]{3,2,1,0:T(8,128)S(1)}, u32[]{:S(2)}, u32[]{:S(2)}) %collective-permute-start.4) | collective-permute-done | bytes 8224 | tf_op jit(solution)/shard_map/ppermute | solution.py:450
  83.6 0.7 broadcast_in_dim.20
  84.3 7.6 %all-to-all-start = ((f32[16,2,8,128]{3,2,1,0:T(8,128)}), f32[16,2,8,128]{3,2,1,0:T(8,128)S(1)}, u32[]{:S(2)}, u32[]{:S(2)}) async-start(f32[16,2,8,128]{3,2,1,0:T(8,128)} %broadcast_in_dim.20), calls=%async_computation.1 | async-start | bytes 262144 | tf_op jit(solution)/shard_map/all_to_all | solution.py:454
  91.9 0.1 dynamic_slice.7
  92.0 0.1 broadcast_in_dim_tile.3.modes_ref
  92.0 8.6 %carry.1.carry_ref = f32[6,16,8,128]{3,2,1,0:T(8,128)S(1)} custom-call(f32[2048]{0:T(1024)S(1)} %get-tuple-element.31.low_ref, f32[2048]{0:T(1024)S(1)} %get-tuple-element.32.up_ref, s32[1,128]{1,0:T(1,128)S(1)} %broadcast_in_dim_tile.3.modes_ref), custom_call_target="tpu_custom_call" | custom-call | tf_op jit(solution)/shard_map/carry/pallas_call | solution.py:458
  100.7 1.7 %own_factors.1 = (f32[128,8,128]{2,1,0:T(8,128)S(1)}, f32[128,8,128]{2,1,0:T(8,128)S(1)}, f32[128,8,128]{2,1,0:T(8,128)S(1)}) custom-call(s32[3]{0:T(128)S(1)} %pad_add_fusion.info_ref, f32[2048]{0:T(1024)S(1)} %get-tuple-element.31.low_ref, f32[2048]{0:T(1024)S(1)} %get-tuple-element.32.up_ref, s32[1,128]{1,0:T(1,128)S(1)} %broadcast_in_dim_tile.3.modes_ref), custom_call_target="tpu_custom_call" | custom-call | tf_op jit(solution)/shard_map/own_factors/pallas_call | solution.py:481
  102.3 0.0 all-to-all-done.ends_ref
  102.3 0.9 interfaces.1.edge_ref
  103.2 26.6 %reduce-scatter.2.cloned.1.call-done.sums_ref = f32[1024,128]{1,0:T(8,128)} async-done(((f32[16384,128]{1,0:T(8,128)}), f32[1024,128]{1,0:T(8,128)}) %reduce-scatter.2.cloned.1.call-update) | async-done | bytes 524304 | tf_op jit(solution)/shard_map/reduce_scatter | solution.py:409
  129.8 2.5 %solve.1 = f32[2,32,16,128]{3,2,1,0:T(8,128)} custom-call(f32[1024,128]{1,0:T(8,128)} %reduce-scatter.2.cloned.1.call-done.sums_ref, f32[2,8,128]{2,1,0:T(8,128)S(1)} %interfaces.1.edge_ref, f32[128,8,128]{2,1,0:T(8,128)S(1)} %get-tuple-element.26.ratio_ref, f32[128,8,128]{2,1,0:T(8,128)S(1)} %get-tuple-element.27.inverse_ref, ...), custom_call_target="tpu_custom_call" | custom-call | tf_op jit(solution)/shard_map/solve/pallas_call | solution.py:491
  (15 shorter events, 0.1 us)
Async XLA Ops:
  6.5 123.3 %reduce-scatter.2.cloned.1.call-start = ((), (), s32[]{:S(2)}) async-start(), calls=%async_computation.2 | async-start | bytes 8912896 | tf_op jit(solution)/shard_map/reduce_scatter | solution.py:409
  6.5 6.3 %collective-permute-start = (f32[32,128,128]{2,1,0:T(8,128)}, f32[32,128,128]{2,1,0:T(8,128)S(1)}, u32[]{:S(2)}, u32[]{:S(2)}) collective-permute-start(f32[32,128,128]{2,1,0:T(8,128)} %own_ref.1), channel_id=1, source_target_pairs={{0,16},{16,0},{32,48},{48,32},{64,80},{80,64},{96,112},{112,96},{1... | collective-permute-start | bytes 6291464 | tf_op jit(solution)/shard_map/ppermute | solution.py:372
  17.7 0.7 copy-start
  17.7 0.9 copy-start.1
  39.7 8.0 %collective-permute-start.1 = (f32[8,2,8,128]{3,2,1,0:T(8,128)S(1)}, f32[8,2,8,128]{3,2,1,0:T(8,128)S(1)}, u32[]{:S(2)}, u32[]{:S(2)}) collective-permute-start(f32[8,2,8,128]{3,2,1,0:T(8,128)S(1)} %slice_bitcast_fusion), channel_id=1, source_target_pairs={{0,32},{16,48},{32,0},{48,16},{64,96},{80,112},{96,64},{112,80},{1... | collective-permute-start | bytes 196616 | tf_op jit(solution)/shard_map/ppermute | solution.py:450
  47.7 8.0 %collective-permute-start.2 = (f32[4,2,8,128]{3,2,1,0:T(8,128)S(1)}, f32[4,2,8,128]{3,2,1,0:T(8,128)S(1)}, u32[]{:S(2)}, u32[]{:S(2)}) collective-permute-start(f32[4,2,8,128]{3,2,1,0:T(8,128)S(1)} %slice_bitcast_fusion.2), channel_id=1, source_target_pairs={{0,64},{16,80},{32,96},{48,112},{64,0},{80,16},{96,32},{112,48},{1... | collective-permute-start | bytes 98312 | tf_op jit(solution)/shard_map/ppermute | solution.py:450
  55.7 11.1 %collective-permute-start.3 = (f32[2,2,8,128]{3,2,1,0:T(8,128)S(1)}, f32[2,2,8,128]{3,2,1,0:T(8,128)S(1)}, u32[]{:S(2)}, u32[]{:S(2)}) collective-permute-start(f32[2,2,8,128]{3,2,1,0:T(8,128)S(1)} %slice_bitcast_fusion.4), channel_id=1, source_target_pairs={{0,128},{16,144},{32,160},{48,176},{64,192},{80,208},{96,224},{112... | collective-permute-start | bytes 49160 | tf_op jit(solution)/shard_map/ppermute | solution.py:450
  66.8 16.8 %collective-permute-start.4 = (f32[1,2,8,128]{3,2,1,0:T(8,128)S(1)}, f32[1,2,8,128]{3,2,1,0:T(8,128)S(1)}, u32[]{:S(2)}, u32[]{:S(2)}) collective-permute-start(f32[1,2,8,128]{3,2,1,0:T(8,128)S(1)} %slice_bitcast_fusion.6), channel_id=1, source_target_pairs={{0,256},{16,272},{32,288},{48,304},{64,320},{80,336},{96,352},{112... | collective-permute-start | bytes 24584 | tf_op jit(solution)/shard_map/ppermute | solution.py:450
  84.3 18.0 %all-to-all-start = ((f32[16,2,8,128]{3,2,1,0:T(8,128)}), f32[16,2,8,128]{3,2,1,0:T(8,128)S(1)}, u32[]{:S(2)}, u32[]{:S(2)}) async-start(f32[16,2,8,128]{3,2,1,0:T(8,128)} %broadcast_in_dim.20), calls=%async_computation.1 | async-start | bytes 262144 | tf_op jit(solution)/shard_map/all_to_all | solution.py:454
Sparse Core Ops, SparseCore 0:
  17.9 111.9 reduce-scatter.1
